TPU v7x, 256 devices: a whole 4x4x8 slice. The times are simulated.
256 devices in a mesh: gx: 16 (over y_hi, x, core), gy: 16 (over z, y_lo).
Axes of the slice: x: 4, y: 4 (y_hi: 2, y_lo: 2; y = y_hi * 2 + y_lo), z: 8, core: 2. Of those that a mesh axis runs over, the one named last changes fastest.
Arguments:
- state: float32 [9, 4, 256, 2048], P(None, None, 'gy', 'gx'), may hold values from -3 to 11, as said below
- inflow: float32 [9, 4, 256, 8], P(None, None, 'gy'), may hold values from -3 to 11, as said below
Outputs:
- advanced: float32 [9, 4, 256, 2048], P(None, None, 'gy', 'gx')
Inputs may be any that keep to these rules, and one draw needn't show every extreme that they name: Every cell is a physical state: density and pressure between 0.5 and 1.8, each species density between 0 and the density. `inflow`: every cell is a physical state: density and pressure between 0.5 and 1.8, each species density between 0 and the density.
All inputs are finite; a program needn't handle non-finite values.
Results may differ from a plain program's by a relative error of at most 0.00002.
Values sent between devices are 32-bit elements; how exact they have to be, the bound alone decides.
A program may use at most 64 MiB of HBM per device.

v0:
```python
import jax
import jax.numpy as jnp
from jax import lax
from jax.sharding import PartitionSpec as P

SHIFT = 8
SUBSTEPS = 4


GAMMA = 1.4
HEAT = 1.0
PREFACTOR = 300.0
ACTIVATION = 4.0
COURANT = 0.15
WENO_EPS = 1e-06


def extended(block, sides, width):
    for axis, dim in sides:
        count = lax.axis_size(axis)
        forward = [(i, i + 1) for i in range(count - 1)]
        forward.append((count - 1, 0))
        backward = [(target, source) for source, target in forward]
        low = lax.ppermute(
            lax.slice_in_dim(block, block.shape[dim] - width, None, axis=dim), axis, forward
        )
        high = lax.ppermute(lax.slice_in_dim(block, 0, width, axis=dim), axis, backward)
        block = jnp.concatenate([low, block, high], axis=dim)
    return block


def shifted_2(block, axis, distance):
    devices = range(lax.axis_size(axis))
    route = [(i - distance, i) for i in devices if i - distance in devices]
    return lax.ppermute(block, axis, route)


def pressure(state):
    density = state[0]
    kinetic = 0.5 * (state[1] * state[1] + state[2] * state[2] + state[3] * state[3]) / density
    return (GAMMA - 1.0) * (state[4] - kinetic - HEAT * state[5])


def wave_speed(state):
    density = state[0]
    sound = jnp.sqrt(GAMMA * pressure(state) / density)
    fastest = (
        jnp.maximum(jnp.maximum(jnp.abs(state[1]), jnp.abs(state[2])), jnp.abs(state[3])) / density
    )
    return jnp.max(fastest + sound)


def flux(state, component):
    velocity = state[component] / state[0]
    press = pressure(state)
    moved = [velocity * state[index] for index in range(9)]
    moved[component] = moved[component] + press
    moved[4] = moved[4] + velocity * press
    return jnp.stack(moved)


def weno(far_left, near_left, centre, near_right, far_right):
    smooth_zero = (
        13.0 / 12.0 * (far_left - 2.0 * near_left + centre) ** 2
        + 0.25 * (far_left - 4.0 * near_left + 3.0 * centre) ** 2
    )
    smooth_one = (
        13.0 / 12.0 * (near_left - 2.0 * centre + near_right) ** 2
        + 0.25 * (near_left - near_right) ** 2
    )
    smooth_two = (
        13.0 / 12.0 * (centre - 2.0 * near_right + far_right) ** 2
        + 0.25 * (3.0 * centre - 4.0 * near_right + far_right) ** 2
    )
    weight_zero = 0.1 / (WENO_EPS + smooth_zero) ** 2
    weight_one = 0.6 / (WENO_EPS + smooth_one) ** 2
    weight_two = 0.3 / (WENO_EPS + smooth_two) ** 2
    guess_zero = (2.0 * far_left - 7.0 * near_left + 11.0 * centre) / 6.0
    guess_one = (-near_left + 5.0 * centre + 2.0 * near_right) / 6.0
    guess_two = (2.0 * centre + 5.0 * near_right - far_right) / 6.0
    return (weight_zero * guess_zero + weight_one * guess_one + weight_two * guess_two) / (
        weight_zero + weight_one + weight_two
    )


def interface_sum(plus, minus, axis, count):

    def part(array, start):
        return lax.slice_in_dim(array, start, start + count + 1, axis=axis)

    faces = weno(part(plus, 0), part(plus, 1), part(plus, 2), part(plus, 3), part(plus, 4))
    faces = faces + weno(
        part(minus, 5), part(minus, 4), part(minus, 3), part(minus, 2), part(minus, 1)
    )
    return lax.slice_in_dim(faces, 1, count + 1, axis=axis) - lax.slice_in_dim(
        faces, 0, count, axis=axis
    )


def directional(block, component, axis, speed):
    count = block.shape[axis] - 6
    read = flux(block, component)
    plus = 0.5 * (read + speed * block)
    minus = 0.5 * (read - speed * block)
    return interface_sum(plus, minus, axis, count)


def rates(padded, speed):
    rows = padded[:, :, 3:-3, :]
    columns = padded[:, :, :, 3:-3]
    core = padded[:, :, 3:-3, 3:-3]
    layers = jnp.concatenate([core[:, -3:], core, core[:, :3]], axis=1)
    total = (
        directional(rows, 1, 3, speed)
        + directional(columns, 2, 2, speed)
        + directional(layers, 3, 1, speed)
    )
    return -total


def react(state, step):
    small = step / SUBSTEPS
    for substep in range(SUBSTEPS):
        temper = pressure(state) / state[0]
        burned = small * PREFACTOR * state[5] * jnp.exp(-ACTIVATION / temper)
        state = jnp.concatenate(
            [state[:5], (state[5] - burned)[None], (state[6] + burned)[None], state[7:]], axis=0
        )
    return state


def fix_ends(padded, margin):
    first_slab = lax.axis_index("gx") == 0
    last_slab = lax.axis_index("gx") == lax.axis_size("gx") - 1
    length = padded.shape[3]
    position = lax.broadcasted_iota(jnp.int32, (1, 1, 1, length), 3)
    lower = padded[..., margin : margin + 1]
    upper = padded[..., length - margin - 1 : length - margin]
    padded = jnp.where(first_slab & (position < margin), lower, padded)
    return jnp.where(last_slab & (position >= length - margin), upper, padded)


def extend(field):
    along_x = extended(field, (("gx", 3),), 3)
    along_y = extended(field, (("gy", 2),), 3)
    padded = jnp.pad(along_y, ((0, 0), (0, 0), (0, 0), (3, 3)))
    padded = padded.at[:, :, 3:-3, :].set(along_x)
    return fix_ends(padded, 3)


def advance(state, inflow):
    last_slab = lax.axis_index("gx") == lax.axis_size("gx") - 1
    arriving = shifted_2(state[..., :SHIFT], "gx", -1)
    return jnp.concatenate([state[..., SHIFT:], jnp.where(last_slab, inflow, arriving)], axis=3)


def global_speed(shifted):
    return lax.pmax(wave_speed(shifted), ("gx", "gy"))


def on_device(state, inflow):
    shifted = advance(state, inflow)
    opening = extend(shifted)
    speed = global_speed(shifted)
    step = COURANT / speed
    first = shifted + step * rates(opening, speed)
    second = 0.75 * shifted + 0.25 * (first + step * rates(extend(first), speed))
    third = shifted / 3.0 + 2.0 / 3.0 * (second + step * rates(extend(second), speed))
    return react(third, step)


def solution(mesh):
    in_specs = (P(None, None, "gy", "gx"), P(None, None, "gy", None))
    out_specs = P(None, None, "gy", "gx")
    return jax.shard_map(
        on_device, mesh=mesh, in_specs=in_specs, out_specs=out_specs, check_vma=False
    )
```

profile of v0, /device:TPU:24, one launch (start us, length us, event | category | flops | bytes accessed | tf_op | source)
XLA Modules:
  0.0 176.8 jit_solution(16806353113119119489)
XLA Ops:
  0.0 4.9 %collective-permute-start = (f32[9,4,16,8]{3,2,1,0:T(8,128)}, f32[9,4,16,8]{3,2,1,0:T(8,128)S(1)}, u32[]{:S(2)}, u32[]{:S(2)}) collective-permute-start(f32[9,4,16,8]{3,2,1,0:T(8,128)} %bitcast.43), channel_id=1, source_target_pairs={{16,0},{32,16},{48,32},{64,48},{80,64},{96,80},{112,96},{128,112},... | collective-permute-start | bytes 55304 | tf_op jit(solution)/shard_map/ppermute | solution.py:35
  4.9 1.1 slice.1014
  7.8 1.6 collective-permute-done
  10.6 2.9 %collective-permute-start.1 = (f32[9,4,3,128]{3,2,1,0:T(4,128)S(1)}, f32[9,4,3,128]{3,2,1,0:T(4,128)S(1)}, u32[]{:S(2)}, u32[]{:S(2)}) collective-permute-start(f32[9,4,3,128]{3,2,1,0:T(4,128)S(1)} %get-tuple-element.109), channel_id=1, source_target_pairs={{0,1},{1,2},{2,3},{3,4},{4,5},{5,6},{6,7},{7,8},{8,9},{9,10},{10,1... | collective-permute-start | bytes 165896 | tf_op jit(solution)/shard_map/ppermute | solution.py:24
  13.5 80.4 %pmax.7 = f32[]{:T(128)} all-reduce(f32[]{:T(128)} %fusion.44), channel_id=1, replica_groups=mesh['gx'=16,'gy'=16] {'gx','gy'}, use_global_device_ids=true, to_apply=%region_1.2 | all-reduce | flops 1 | bytes 8 | tf_op jit(solution)/shard_map/pmax | solution.py:158
  95.8 5.4 %scatter.10 = f32[9,4,22,134]{3,2,1,0:T(8,128)S(1)} dynamic-update-slice(f32[9,4,22,134]{3,2,1,0:T(8,128)S(1)} %select_maximum_fusion.4, f32[9,4,16,134]{3,2,1,0:T(8,128)S(1)} %pad_maximum_fusion.3, s32[]{:T(128)} %constant.205.clone.1, s32[]{:T(128)} %constant.205.clone.1, s32[]{:T(128)} %constant.206.clone.1, s32[]{:T(128)} %constant.205.clone.1) | dynamic-update-slice | bytes 617476 | tf_op jit(solution)/shard_map/scatter | solution.py:147
  102.9 0.8 add_multiply_fusion.2
  104.5 0.9 add_multiply_fusion.8
  105.5 0.8 add_multiply_fusion.5
  106.4 1.6 divide_add_fusion.8
  108.0 2.3 %divide_add_fusion.5 = f32[9,4,17,128]{3,2,1,0:T(8,128)S(1)} fusion(f32[9,4,22,128]{3,2,1,0:T(8,128)S(1)} %get-tuple-element.102, f32[9,4,22,128]{3,2,1,0:T(8,128)S(1)} %get-tuple-element.101), kind=kLoop, calls=%fused_computation.52 | loop fusion | flops 10105344 | bytes 3446784 | tf_op jit(solution)/shard_map/add | solution.py:92
  110.3 3.0 %divide_add_fusion.2 = f32[9,4,16,129]{3,2,1,0:T(8,128)S(1)} fusion(f32[9,4,16,134]{3,2,1,0:T(8,128)S(1)} %get-tuple-element.94, f32[9,4,16,134]{3,2,1,0:T(8,128)S(1)} %get-tuple-element.93), kind=kLoop, calls=%fused_computation.34 | loop fusion | flops 9585216 | bytes 3269376 | tf_op jit(solution)/shard_map/add | solution.py:92
  113.7 3.2 %collective-permute-start.8 = (f32[9,4,16,3]{3,2,1,0:T(8,128)S(1)}, f32[9,4,16,3]{3,2,1,0:T(8,128)S(1)}, u32[]{:S(2)}, u32[]{:S(2)}) collective-permute-start(f32[9,4,16,3]{3,2,1,0:T(8,128)S(1)} %get-tuple-element.116), channel_id=1, source_target_pairs={{16,0},{32,16},{48,32},{64,48},{80,64},{96,80},{112,96},{128,112},... | collective-permute-start | bytes 20744 | tf_op jit(solution)/shard_map/ppermute | solution.py:27
  116.9 2.9 %collective-permute-start.5 = (f32[9,4,3,128]{3,2,1,0:T(4,128)S(1)}, f32[9,4,3,128]{3,2,1,0:T(4,128)S(1)}, u32[]{:S(2)}, u32[]{:S(2)}) collective-permute-start(f32[9,4,3,128]{3,2,1,0:T(4,128)S(1)} %get-tuple-element.117), channel_id=1, source_target_pairs={{0,1},{1,2},{2,3},{3,4},{4,5},{5,6},{6,7},{7,8},{8,9},{9,10},{10,1... | collective-permute-start | bytes 165896 | tf_op jit(solution)/shard_map/ppermute | solution.py:24
  119.9 2.0 %collective-permute-done.8 = f32[9,4,16,3]{3,2,1,0:T(8,128)S(1)} collective-permute-done((f32[9,4,16,3]{3,2,1,0:T(8,128)S(1)}, f32[9,4,16,3]{3,2,1,0:T(8,128)S(1)}, u32[]{:S(2)}, u32[]{:S(2)}) %collective-permute-start.8) | collective-permute-done | bytes 6944 | tf_op jit(solution)/shard_map/ppermute | solution.py:27
  121.9 5.4 %collective-permute-done.7 = f32[9,4,16,3]{3,2,1,0:T(8,128)S(1)} collective-permute-done((f32[9,4,16,3]{3,2,1,0:T(8,128)S(1)}, f32[9,4,16,3]{3,2,1,0:T(8,128)S(1)}, u32[]{:S(2)}, u32[]{:S(2)}) %collective-permute-start.7) | collective-permute-done | bytes 6944 | tf_op jit(solution)/shard_map/ppermute | solution.py:24
  128.1 5.4 %scatter.11 = f32[9,4,22,134]{3,2,1,0:T(8,128)S(1)} dynamic-update-slice(f32[9,4,22,134]{3,2,1,0:T(8,128)S(1)} %select_maximum_fusion.2, f32[9,4,16,134]{3,2,1,0:T(8,128)S(1)} %pad_maximum_fusion.4, s32[]{:T(128)} %constant.205.clone.1, s32[]{:T(128)} %constant.205.clone.1, s32[]{:T(128)} %constant.206.clone.1, s32[]{:T(128)} %constant.205.clone.1) | dynamic-update-slice | bytes 617476 | tf_op jit(solution)/shard_map/scatter | solution.py:147
  136.7 0.9 add_multiply_fusion.7
  137.8 0.8 add_multiply_fusion.4
  138.7 1.6 divide_add_fusion.7
  140.3 2.3 %divide_add_fusion.4 = f32[9,4,17,128]{3,2,1,0:T(8,128)S(1)} fusion(f32[9,4,22,128]{3,2,1,0:T(8,128)S(1)} %get-tuple-element.100, f32[9,4,22,128]{3,2,1,0:T(8,128)S(1)} %get-tuple-element.99), kind=kLoop, calls=%fused_computation.49 | loop fusion | flops 10105344 | bytes 3446784 | tf_op jit(solution)/shard_map/add | solution.py:92
  142.6 3.0 %divide_add_fusion.1 = f32[9,4,16,129]{3,2,1,0:T(8,128)S(1)} fusion(f32[9,4,16,134]{3,2,1,0:T(8,128)S(1)} %get-tuple-element.90, f32[9,4,16,134]{3,2,1,0:T(8,128)S(1)} %get-tuple-element.89), kind=kLoop, calls=%fused_computation.31 | loop fusion | flops 9585216 | bytes 3269376 | tf_op jit(solution)/shard_map/add | solution.py:92
  146.9 2.9 %collective-permute-start.9 = (f32[9,4,3,128]{3,2,1,0:T(4,128)S(1)}, f32[9,4,3,128]{3,2,1,0:T(4,128)S(1)}, u32[]{:S(2)}, u32[]{:S(2)}) collective-permute-start(f32[9,4,3,128]{3,2,1,0:T(4,128)S(1)} %get-tuple-element.113), channel_id=1, source_target_pairs={{0,1},{1,2},{2,3},{3,4},{4,5},{5,6},{6,7},{7,8},{8,9},{9,10},{10,1... | collective-permute-start | bytes 165896 | tf_op jit(solution)/shard_map/ppermute | solution.py:24
  149.8 1.9 %collective-permute-done.12 = f32[9,4,16,3]{3,2,1,0:T(8,128)S(1)} collective-permute-done((f32[9,4,16,3]{3,2,1,0:T(8,128)S(1)}, f32[9,4,16,3]{3,2,1,0:T(8,128)S(1)}, u32[]{:S(2)}, u32[]{:S(2)}) %collective-permute-start.12) | collective-permute-done | bytes 6944 | tf_op jit(solution)/shard_map/ppermute | solution.py:27
  151.7 5.6 %collective-permute-done.11 = f32[9,4,16,3]{3,2,1,0:T(8,128)S(1)} collective-permute-done((f32[9,4,16,3]{3,2,1,0:T(8,128)S(1)}, f32[9,4,16,3]{3,2,1,0:T(8,128)S(1)}, u32[]{:S(2)}, u32[]{:S(2)}) %collective-permute-start.11) | collective-permute-done | bytes 6944 | tf_op jit(solution)/shard_map/ppermute | solution.py:24
  158.1 5.4 %scatter.14 = f32[9,4,22,134]{3,2,1,0:T(8,128)S(1)} dynamic-update-slice(f32[9,4,22,134]{3,2,1,0:T(8,128)S(1)} %select_maximum_fusion, f32[9,4,16,134]{3,2,1,0:T(8,128)S(1)} %pad_maximum_fusion.5, s32[]{:T(128)} %constant.205.clone.1, s32[]{:T(128)} %constant.205.clone.1, s32[]{:T(128)} %constant.206.clone.1, s32[]{:T(128)} %constant.205.clone.1) | dynamic-update-slice | bytes 617476 | tf_op jit(solution)/shard_map/scatter | solution.py:147
  165.1 0.8 add_multiply_fusion
  166.7 0.9 add_multiply_fusion.6
  167.8 0.8 add_multiply_fusion.3
  168.6 1.6 divide_add_fusion.6
  170.3 2.3 %divide_add_fusion.3 = f32[9,4,17,128]{3,2,1,0:T(8,128)S(1)} fusion(f32[9,4,22,128]{3,2,1,0:T(8,128)S(1)} %get-tuple-element.98, f32[9,4,22,128]{3,2,1,0:T(8,128)S(1)} %get-tuple-element.97), kind=kLoop, calls=%fused_computation.46 | loop fusion | flops 10105344 | bytes 3446784 | tf_op jit(solution)/shard_map/add | solution.py:92
  172.5 3.0 %divide_add_fusion = f32[9,4,16,129]{3,2,1,0:T(8,128)S(1)} fusion(f32[9,4,16,134]{3,2,1,0:T(8,128)S(1)} %get-tuple-element.86, f32[9,4,16,134]{3,2,1,0:T(8,128)S(1)} %get-tuple-element.85), kind=kLoop, calls=%fused_computation.28 | loop fusion | flops 9585216 | bytes 3269376 | tf_op jit(solution)/shard_map/add | solution.py:92
  (142 shorter events, 16.8 us)
Async XLA Ops:
  0.0 6.8 %copy-start = (f32[9,4,16,128]{3,2,1,0:T(8,128)S(1)}, f32[9,4,16,128]{3,2,1,0:T(8,128)}, u32[]{:S(2)}) copy-start(f32[9,4,16,128]{3,2,1,0:T(8,128)} %param.8) | copy-start | bytes 884740
  0.0 9.4 %collective-permute-start = (f32[9,4,16,8]{3,2,1,0:T(8,128)}, f32[9,4,16,8]{3,2,1,0:T(8,128)S(1)}, u32[]{:S(2)}, u32[]{:S(2)}) collective-permute-start(f32[9,4,16,8]{3,2,1,0:T(8,128)} %bitcast.43), channel_id=1, source_target_pairs={{16,0},{32,16},{48,32},{64,48},{80,64},{96,80},{112,96},{128,112},... | collective-permute-start | bytes 55304 | tf_op jit(solution)/shard_map/ppermute | solution.py:35
  6.0 88.6 %collective-permute-start.4 = (f32[9,4,16,3]{3,2,1,0:T(8,128)S(1)}, f32[9,4,16,3]{3,2,1,0:T(8,128)S(1)}, u32[]{:S(2)}, u32[]{:S(2)}) collective-permute-start(f32[9,4,16,3]{3,2,1,0:T(8,128)S(1)} %slice.1014), channel_id=1, source_target_pairs={{16,0},{32,16},{48,32},{64,48},{80,64},{96,80},{112,96},{128,112},... | collective-permute-start | bytes 20744 | tf_op jit(solution)/shard_map/ppermute | solution.py:27
  6.8 0.9 copy-start.1
  9.8 84.9 %collective-permute-start.3 = (f32[9,4,16,3]{3,2,1,0:T(8,128)S(1)}, f32[9,4,16,3]{3,2,1,0:T(8,128)S(1)}, u32[]{:S(2)}, u32[]{:S(2)}) collective-permute-start(f32[9,4,16,3]{3,2,1,0:T(8,128)S(1)} %slice.1258), channel_id=1, source_target_pairs={{0,16},{16,32},{32,48},{48,64},{64,80},{80,96},{96,112},{112,128},... | collective-permute-start | bytes 20744 | tf_op jit(solution)/shard_map/ppermute | solution.py:24
  10.6 84.5 %collective-permute-start.2 = (f32[9,4,3,128]{3,2,1,0:T(4,128)S(1)}, f32[9,4,3,128]{3,2,1,0:T(4,128)S(1)}, u32[]{:S(2)}, u32[]{:S(2)}) collective-permute-start(f32[9,4,3,128]{3,2,1,0:T(4,128)S(1)} %get-tuple-element.110), channel_id=1, source_target_pairs={{1,0},{2,1},{3,2},{4,3},{5,4},{6,5},{7,6},{8,7},{9,8},{10,9},{11,1... | collective-permute-start | bytes 165896 | tf_op jit(solution)/shard_map/ppermute | solution.py:27
  10.6 84.5 %collective-permute-start.1 = (f32[9,4,3,128]{3,2,1,0:T(4,128)S(1)}, f32[9,4,3,128]{3,2,1,0:T(4,128)S(1)}, u32[]{:S(2)}, u32[]{:S(2)}) collective-permute-start(f32[9,4,3,128]{3,2,1,0:T(4,128)S(1)} %get-tuple-element.109), channel_id=1, source_target_pairs={{0,1},{1,2},{2,3},{3,4},{4,5},{5,6},{6,7},{7,8},{8,9},{9,10},{10,1... | collective-permute-start | bytes 165896 | tf_op jit(solution)/shard_map/ppermute | solution.py:24
  113.7 8.2 %collective-permute-start.8 = (f32[9,4,16,3]{3,2,1,0:T(8,128)S(1)}, f32[9,4,16,3]{3,2,1,0:T(8,128)S(1)}, u32[]{:S(2)}, u32[]{:S(2)}) collective-permute-start(f32[9,4,16,3]{3,2,1,0:T(8,128)S(1)} %get-tuple-element.116), channel_id=1, source_target_pairs={{16,0},{32,16},{48,32},{64,48},{80,64},{96,80},{112,96},{128,112},... | collective-permute-start | bytes 20744 | tf_op jit(solution)/shard_map/ppermute | solution.py:27
  116.8 10.5 %collective-permute-start.7 = (f32[9,4,16,3]{3,2,1,0:T(8,128)S(1)}, f32[9,4,16,3]{3,2,1,0:T(8,128)S(1)}, u32[]{:S(2)}, u32[]{:S(2)}) collective-permute-start(f32[9,4,16,3]{3,2,1,0:T(8,128)S(1)} %get-tuple-element.115), channel_id=1, source_target_pairs={{0,16},{16,32},{32,48},{48,64},{64,80},{80,96},{96,112},{112,128},... | collective-permute-start | bytes 20744 | tf_op jit(solution)/shard_map/ppermute | solution.py:24
  116.9 10.8 %collective-permute-start.6 = (f32[9,4,3,128]{3,2,1,0:T(4,128)S(1)}, f32[9,4,3,128]{3,2,1,0:T(4,128)S(1)}, u32[]{:S(2)}, u32[]{:S(2)}) collective-permute-start(f32[9,4,3,128]{3,2,1,0:T(4,128)S(1)} %get-tuple-element.118), channel_id=1, source_target_pairs={{1,0},{2,1},{3,2},{4,3},{5,4},{6,5},{7,6},{8,7},{9,8},{10,9},{11,1... | collective-permute-start | bytes 165896 | tf_op jit(solution)/shard_map/ppermute | solution.py:27
  116.9 10.7 %collective-permute-start.5 = (f32[9,4,3,128]{3,2,1,0:T(4,128)S(1)}, f32[9,4,3,128]{3,2,1,0:T(4,128)S(1)}, u32[]{:S(2)}, u32[]{:S(2)}) collective-permute-start(f32[9,4,3,128]{3,2,1,0:T(4,128)S(1)} %get-tuple-element.117), channel_id=1, source_target_pairs={{0,1},{1,2},{2,3},{3,4},{4,5},{5,6},{6,7},{7,8},{8,9},{9,10},{10,1... | collective-permute-start | bytes 165896 | tf_op jit(solution)/shard_map/ppermute | solution.py:24
  146.0 5.8 %collective-permute-start.12 = (f32[9,4,16,3]{3,2,1,0:T(8,128)S(1)}, f32[9,4,16,3]{3,2,1,0:T(8,128)S(1)}, u32[]{:S(2)}, u32[]{:S(2)}) collective-permute-start(f32[9,4,16,3]{3,2,1,0:T(8,128)S(1)} %get-tuple-element.112), channel_id=1, source_target_pairs={{16,0},{32,16},{48,32},{64,48},{80,64},{96,80},{112,96},{128,112},... | collective-permute-start | bytes 20744 | tf_op jit(solution)/shard_map/ppermute | solution.py:27
  146.8 10.6 %collective-permute-start.11 = (f32[9,4,16,3]{3,2,1,0:T(8,128)S(1)}, f32[9,4,16,3]{3,2,1,0:T(8,128)S(1)}, u32[]{:S(2)}, u32[]{:S(2)}) collective-permute-start(f32[9,4,16,3]{3,2,1,0:T(8,128)S(1)} %get-tuple-element.111), channel_id=1, source_target_pairs={{0,16},{16,32},{32,48},{48,64},{64,80},{80,96},{96,112},{112,128},... | collective-permute-start | bytes 20744 | tf_op jit(solution)/shard_map/ppermute | solution.py:24
  146.8 10.8 %collective-permute-start.10 = (f32[9,4,3,128]{3,2,1,0:T(4,128)S(1)}, f32[9,4,3,128]{3,2,1,0:T(4,128)S(1)}, u32[]{:S(2)}, u32[]{:S(2)}) collective-permute-start(f32[9,4,3,128]{3,2,1,0:T(4,128)S(1)} %get-tuple-element.114), channel_id=1, source_target_pairs={{1,0},{2,1},{3,2},{4,3},{5,4},{6,5},{7,6},{8,7},{9,8},{10,9},{11,1... | collective-permute-start | bytes 165896 | tf_op jit(solution)/shard_map/ppermute | solution.py:27
  146.9 10.7 %collective-permute-start.9 = (f32[9,4,3,128]{3,2,1,0:T(4,128)S(1)}, f32[9,4,3,128]{3,2,1,0:T(4,128)S(1)}, u32[]{:S(2)}, u32[]{:S(2)}) collective-permute-start(f32[9,4,3,128]{3,2,1,0:T(4,128)S(1)} %get-tuple-element.113), channel_id=1, source_target_pairs={{0,1},{1,2},{2,3},{3,4},{4,5},{5,6},{6,7},{7,8},{8,9},{9,10},{10,1... | collective-permute-start | bytes 165896 | tf_op jit(solution)/shard_map/ppermute | solution.py:24
where the time goes:
time: 177 us
  blocking collectives  80.4 us (45%)
  other arithmetic  38 us (21%)
  local copies, waits for them, and re-layouts  21.5 us (12%)
  starting transfers between devices  18.6 us (11%)
  waiting for transfers between devices  16.6 us (9%)
    pmax x1, blocking collectives, global_speed(): return lax.pmax(wave_speed(shifted), ('gx', 'gy'))  80.4 us
    add x9, other arithmetic, interface_sum(): faces + weno(part(minus, 5), part(minus, 4), part(minus, 3), part(minus,...  20.6 us
    scatter x3, local copies, waits for them, and re-layouts, extend(): padded = padded.at[:, :, 3:-3, :].set(along_x)  16.1 us
    ppermute x6, waiting for transfers between devices, extended(): lax.ppermute(lax.slice_in_dim(block, block.shape[dim] - width, None, axis...  11 us
    ppermute x6, starting transfers between devices, extended(): lax.ppermute(lax.slice_in_dim(block, block.shape[dim] - width, None, axis...  8.83 us
    mul x9, other arithmetic, directional(): plus = 0.5 * (read + speed * block)  7.54 us
    ppermute x1, starting transfers between devices, shifted_2(): return lax.ppermute(block, axis, route)  4.9 us
    ppermute x6, starting transfers between devices, extended(): lax.ppermute(lax.slice_in_dim(block, 0, width, axis=dim), axis, backward)  4.85 us
  transfers between devices with their start and end apart: 13, of which 5 were waited for; matrix products, arithmetic and copies ran while one was open for 2% of the time, Pallas kernels for 0%

commit v1 on v0

v1 whole, which is shorter than its diff:
```python
import functools

import jax
import jax.numpy as jnp
from jax import lax
from jax.experimental import pallas as pl
from jax.experimental.pallas import tpu as pltpu
from jax.sharding import PartitionSpec as P

MESH = pl.DeviceIdType.MESH
NZ = 4
NY = 16
LANES = 128
COMPS = 9
GROUPS = 8
BLOCKS = 9
SUBSTEPS = 4
PREFACTOR = 300.0
ACTIVATION = 4.0
COURANT = 0.15
EPS = 3e-6
STAGES = ((0.0, 1.0), (0.75, 0.25), (1.0 / 3.0, 2.0 / 3.0))


def reciprocal(x):
    return pltpu.reciprocal(x, approx=True)


def roll(x, shift):
    shift = shift % LANES
    return x if shift == 0 else pltpu.roll(x, shift, axis=1)


def cell_terms(d_low, d_high, q_low, q_high):
    second = d_high - d_low
    cross = d_high * d_low
    squares = (q_low + q_high) + EPS
    base = squares - 2.75 * cross
    r_low = reciprocal(base + 1.5 * q_high)
    r_mid = reciprocal(squares - 1.25 * cross)
    r_high = reciprocal(base + 1.5 * q_low)
    return second, r_low * r_low, 6.0 * (r_mid * r_mid), r_high * r_high


def correction(w_far, w_mid, w_near, t_far, t_near):
    near = 3.0 * w_near
    return (w_far * t_far + near * (0.5 * t_near)) * reciprocal((w_far + w_mid) + near)


def plus_face(g, d_low, d_high, fix):
    return 6.0 * g + d_low + 2.0 * (d_high - fix)


def minus_face(g, d_low, d_high, fix):
    return 6.0 * g - d_high - 2.0 * (d_low - fix)


def stream_faces(load, first, last, emit):
    gp, gm, dp, dm, qp, qm = {}, {}, {}, {}, {}, {}
    tp, tm, sp, sm, wp, wm = {}, {}, {}, {}, {}, {}
    plus = {}
    for j in range(first - 2, last + 4):
        gp[j], gm[j] = load(j)
        k = j - 1
        if j > first - 2:
            dp[k] = gp[j] - gp[k]
            qp[k] = dp[k] * dp[k]
            dm[k] = gm[j] - gm[k]
            qm[k] = dm[k] * dm[k]
        if j >= first:
            sp[k], *wp[k] = cell_terms(dp[k - 1], dp[k], qp[k - 1], qp[k])
            sm[k], *wm[k] = cell_terms(dm[k - 1], dm[k], qm[k - 1], qm[k])
            if k > first - 1:
                tp[k - 1] = sp[k] - sp[k - 1]
                tm[k - 1] = sm[k] - sm[k - 1]
            i = k - 1
            if first <= i <= last:
                fix = correction(wp[i - 1][0], wp[i][1], wp[i + 1][2], tp[i - 1], tp[i])
                plus[i] = plus_face(gp[i], dp[i - 1], dp[i], fix)
            i, c = k - 2, k - 1
            if first <= i <= last:
                fix = correction(wm[c + 1][2], wm[c][1], wm[c - 1][0], tm[c], tm[c - 1])
                emit(i, plus[i] + minus_face(gm[c], dm[c - 1], dm[c], fix))


def ring_differences(gp, gm):
    n = len(gp)

    def up(x):
        return [x[(i + 1) % n] for i in range(n)]

    def down(x):
        return [x[(i - 1) % n] for i in range(n)]

    def parts(g):
        d = [b - a for a, b in zip(g, up(g))]
        q = [a * a for a in d]
        terms = [cell_terms(*each) for each in zip(down(d), d, down(q), q)]
        s, low, mid, high = map(list, zip(*terms))
        t = [b - a for a, b in zip(s, up(s))]
        return d, t, low, mid, high

    d, t, low, mid, high = parts(gp)
    fix = [correction(*each) for each in zip(down(low), mid, up(high), down(t), t)]
    plus = [plus_face(*each) for each in zip(gp, down(d), d, fix)]
    d, t, low, mid, high = parts(gm)
    fix = [correction(*each) for each in zip(up(high), mid, down(low), t, down(t))]
    minus = [minus_face(*each) for each in zip(gm, down(d), d, fix)]
    faces = [a + b for a, b in zip(plus, up(minus))]
    return [a - b for a, b in zip(faces, down(faces))]


def lane_faces(gp, gm):
    def up(x):
        return roll(x, -1)

    def down(x):
        return roll(x, 1)

    def parts(g):
        d_high = up(g) - g
        d_low = down(d_high)
        second, low, mid, high = cell_terms(d_low, d_high, d_low * d_low, d_high * d_high)
        return d_low, d_high, up(second) - second, second - down(second), down(low), mid, up(high)

    d_low, d_high, t_up, t_down, low, mid, high = parts(gp)
    plus = plus_face(gp, d_low, d_high, correction(low, mid, high, t_down, t_up))
    d_low, d_high, t_up, t_down, low, mid, high = parts(gm)
    minus = minus_face(gm, d_low, d_high, correction(high, mid, low, t_up, t_down))
    return plus + up(minus)


def primitives(rho, m1, m2, m3, energy, reactant):
    inverse = reciprocal(rho)
    v1, v2, v3 = m1 * inverse, m2 * inverse, m3 * inverse
    kinetic = 0.5 * (m1 * v1 + m2 * v2 + m3 * v3)
    return v1, v2, v3, 0.4 * (energy - kinetic - reactant)


def signal_speed(rho, m1, m2, m3, energy, reactant):
    press = primitives(rho, m1, m2, m3, energy, reactant)[3]
    inverse = reciprocal(rho)
    fastest = jnp.maximum(jnp.maximum(jnp.abs(m1), jnp.abs(m2)), jnp.abs(m3))
    return fastest * inverse + jnp.sqrt(1.4 * press * inverse)


def kernel(
    nx, ny, state, inflow, out,
    raw, infl, result, fields, cells, prim, halo_prim, flux_p, flux_m, acc, faces,
    windows, edges, ninth_p, ninth_m, ninth_d, pack, from_left, from_right, halo, peak_x, peak_y, consts,
    local_sem, send_sem, recv_sem,
):
    me_x, me_y = lax.axis_index("gx"), lax.axis_index("gy")
    is_first, is_last = me_x == 0, me_x == nx - 1
    lane = lax.broadcasted_iota(jnp.int32, (8, LANES), 1)
    sub = lax.broadcasted_iota(jnp.int32, (8, LANES), 0)
    place = lane & 15

    def peer(dx, dy):
        return (lax.rem(me_x + (dx + nx), nx), lax.rem(me_y + (dy + ny), ny))

    def remote(src, dst, slot, target):
        return pltpu.make_async_remote_copy(
            src_ref=src, dst_ref=dst, send_sem=send_sem.at[slot], recv_sem=recv_sem.at[slot],
            device_id=target, device_id_type=MESH,
        )

    fetch_state = pltpu.make_async_copy(state, raw, local_sem.at[0])
    fetch_inflow = pltpu.make_async_copy(inflow, infl, local_sem.at[1])
    fetch_state.start()
    fetch_inflow.start()
    barrier = pltpu.get_barrier_semaphore()
    for k in range(1, nx):
        pl.semaphore_signal(barrier, inc=1, device_id=peer(k, 0), device_id_type=MESH)
    for k in range(1, ny):
        pl.semaphore_signal(barrier, inc=1, device_id=peer(0, k), device_id_type=MESH)
    fetch_state.wait()
    fetch_inflow.wait()

    def tile_speed(ref, g):
        rows = [ref[pl.ds(64 * c + 8 * g, 8), :] for c in range(6)]
        return signal_speed(*rows)

    peak = tile_speed(raw, 0)
    entering = tile_speed(infl, 0)
    for g in range(1, GROUPS):
        peak = jnp.maximum(peak, tile_speed(raw, g))
        entering = jnp.maximum(entering, tile_speed(infl, g))
    peak = jnp.where(is_first & (lane < 8), 0.0, peak)
    peak_x[pl.ds(0, 8), :] = jnp.maximum(peak, jnp.max(entering))

    pl.semaphore_wait(barrier, nx + ny - 2)

    def spread(buffer, count, base, step):
        copies = []
        for k in range(1, count):
            copies.append(
                remote(buffer.at[pl.ds(0, 8)], buffer.at[pl.ds(8 * k, 8)], base + k, peer(*step(k)))
            )
            copies[-1].start()
        return copies

    def gather(buffer, copies):
        total = buffer[pl.ds(0, 8), :]
        for k, copy in enumerate(copies):
            copy.wait_recv()
            total = jnp.maximum(total, buffer[pl.ds(8 * (k + 1), 8), :])
        return total

    sent_x = spread(peak_x, nx, 0, lambda k: (k, 0))

    def pack_opening(q, _):
        head = jnp.zeros((8, LANES), jnp.float32)
        own = head
        for g in range(GROUPS):
            block = opening_block(raw, g, q)
            here = (lane >> 4) == g
            head = jnp.where(here, roll(block, 16 * g + 5), head)
            own = jnp.where(here, roll(block, 16 * g - 5), own)
        pack[0, pl.ds(pl.multiple_of(8 * q, 8), 8), :] = head
        windows[pl.ds(pl.multiple_of(8 * q, 8), 8), :] = own
        return 0

    def opening_block(ref, g, q):
        if isinstance(q, int) and q == 8:
            return ref[pl.ds(64 * 8 + 8 * g, 8), :]
        return ref[pl.ds(8 * g + q, 8, stride=64), :]

    lax.fori_loop(0, 8, pack_opening, 0)
    pack_opening(8, 0)

    shift_copy = remote(pack.at[0], from_right.at[0], 2 * 16, peer(-1, 0))

    @pl.when(me_x > 0)
    def _():
        shift_copy.start()

    @pl.when(is_last)
    def _():
        def pack_inflow(q, _):
            head = jnp.zeros((8, LANES), jnp.float32)
            for g in range(GROUPS):
                block = opening_block(infl, g, q)
                block = jnp.concatenate([block, jnp.zeros((8, LANES - 8), jnp.float32)], axis=1)
                head = jnp.where((lane >> 4) == g, roll(block, 16 * g + 5), head)
            for k in range(1, 4):
                head = jnp.where(place == 12 + k, roll(head, k), head)
            from_right[0, pl.ds(pl.multiple_of(8 * q, 8), 8), :] = head
            return 0

        lax.fori_loop(0, 8, pack_inflow, 0)
        pack_inflow(8, 0)

    peak_y[pl.ds(0, 8), :] = gather(peak_x, sent_x)
    sent_y = spread(peak_y, ny, 16, lambda k: (0, k))

    @pl.when(jnp.logical_not(is_last))
    def _():
        shift_copy.wait_recv()

    def assemble(q, _):
        rows = pl.ds(pl.multiple_of(8 * q, 8), 8)
        arrived = from_right[0, rows, :]
        for g in range(GROUPS):
            block = opening_block(raw, g, q)
            block = jnp.where(lane < LANES - 8, roll(block, -8), roll(arrived, 115 - 16 * g))
            fields[0, g // 2, g % 2, rows, :] = block
        own = windows[rows, :]
        edge = own
        for k in range(1, 4):
            edge = jnp.where(place == 3 - k, roll(own, -k), edge)
        own = jnp.where(is_first, edge, own)
        windows[rows, :] = jnp.where(place < 8, own, arrived)
        return 0

    lax.fori_loop(0, 8, assemble, 0)
    assemble(8, 0)

    def y_copies(stage):
        now, base = fields.at[stage], 33 + 3 * stage
        low, high = halo.at[stage, 0], halo.at[stage, 1]
        return [
            remote(now.at[:, 1, 40:72, :], low, base, peer(0, 1)),
            remote(now.at[:, 0, 0:24, :], high.at[:, 0:24, :], base + 1, peer(0, -1)),
            remote(now.at[:, 0, 64:72, :], high.at[:, 24:32, :], base + 2, peer(0, -1)),
        ]

    def x_copies(stage):
        base = 42 + 2 * (stage - 1)
        return [
            remote(pack.at[stage], from_left.at[stage], base, peer(1, 0)),
            remote(pack.at[stage], from_right.at[stage], base + 1, peer(-1, 0)),
        ]

    for copy in y_copies(0):
        copy.start()

    top = jnp.max(gather(peak_y, sent_y))
    speed = jnp.full((8, LANES), top, jnp.float32)
    consts[0] = speed
    consts[1] = COURANT / speed

    def fluxes(block, velocity, press, lam, component):
        flow = velocity * (block + jnp.where(sub == 4, press, 0.0))
        flow = flow + jnp.where(sub == component, press, 0.0)
        move = lam * block
        return flow + move, flow - move

    def ninth_fluxes(block, velocity, lam):
        flow, move = velocity * block, lam * block
        return flow + move, flow - move

    for stage in range(3):
        now = fields.at[stage]
        lam = consts[0]

        def own_primitives(g, _):
            z, t = g // 2, g % 2
            rows = [now[z, t, pl.ds(c, 8, stride=8), :] for c in range(6)]
            for index, value in enumerate(primitives(*rows)):
                prim[index, g] = value
            return 0

        lax.fori_loop(0, GROUPS, own_primitives, 0)

        def spanwise(t, _):
            for q in range(BLOCKS):
                rows = pl.ds(8 * q, 8)
                gp, gm = [], []
                for z in range(NZ):
                    block = now[z, t, rows, :]
                    if q < 8:
                        v1, v3, press = (prim[i, 2 * z + t, q : q + 1, :] for i in (0, 2, 3))
                        one = fluxes(block, v1, press, lam, 1)
                        three = fluxes(block, v3, press, lam, 3)
                    else:
                        one = ninth_fluxes(block, prim[0, 2 * z + t], lam)
                        three = ninth_fluxes(block, prim[2, 2 * z + t], lam)
                    flux_p[z, t, rows, :], flux_m[z, t, rows, :] = one
                    gp.append(three[0])
                    gm.append(three[1])
                for z, value in enumerate(ring_differences(gp, gm)):
                    acc[z, t, rows, :] = value
            return 0

        lax.fori_loop(0, 2, spanwise, 0)

        def streamwise(g, _):
            z, t = g // 2, g % 2
            for q in range(BLOCKS):
                rows = pl.ds(8 * q, 8)
                faces[z, t, rows, :] = lane_faces(flux_p[z, t, rows, :], flux_m[z, t, rows, :])
            return 0

        lax.fori_loop(0, GROUPS, streamwise, 0)

        if stage > 0:
            left, right = x_copies(stage)

            @pl.when(me_x > 0)
            def _():
                left.wait_recv()

            @pl.when(jnp.logical_not(is_last))
            def _():
                right.wait_recv()

            for q in range(BLOCKS):
                rows = pl.ds(8 * q, 8)
                own = pack[stage, rows, :]
                low, high = own, own
                for k in range(1, 4):
                    low = jnp.where(place == 3 - k, roll(own, -k), low)
                    high = jnp.where(place == 12 + k, roll(own, k), high)
                low = jnp.where(is_first, low, from_left[stage, rows, :])
                high = jnp.where(is_last, high, from_right[stage, rows, :])
                windows[rows, :] = jnp.where(place < 3, low, jnp.where(place > 12, high, own))

        rows6 = [windows[pl.ds(c, 8, stride=8), :] for c in range(6)]
        v1, _, _, press = primitives(*rows6)
        edges[0, pl.ds(0, 8), :] = v1
        edges[0, pl.ds(8, 8), :] = press
        for q in range(BLOCKS):
            rows = pl.ds(8 * q, 8)
            block = windows[rows, :]
            if q < 8:
                pair = fluxes(block, edges[0, q : q + 1, :], edges[0, 8 + q : 9 + q, :], lam, 1)
            else:
                pair = ninth_fluxes(block, v1, lam)
            h = lane_faces(*pair)
            edges[1, rows, :] = h
            edges[2, rows, :] = jnp.where(place < 3, roll(h, -10), h)

        for copy in y_copies(stage):
            copy.wait_recv()
        for side in range(2):
            for z in range(NZ):
                rows = [halo[stage, side, z, pl.ds(c, 3, stride=8), :] for c in range(6)]
                _, v2, _, press = primitives(*rows)
                start = 5 if side == 0 else 0
                halo_prim[0, side, z, start : start + 3, :] = v2
                halo_prim[1, side, z, start : start + 3, :] = press

        def transverse(z, _):
            def load(j):
                if 0 <= j < NY:
                    t, q = j // 8, j % 8
                    block = now[z, t, pl.ds(8 * q, 8), :]
                    v2, press = (prim[i, 2 * z + t, q : q + 1, :] for i in (1, 3))
                else:
                    side, q = (0, j + 8) if j < 0 else (1, j - NY)
                    block = halo[stage, side, z, pl.ds(8 * (j + 3 if j < 0 else q), 8), :]
                    v2, press = (halo_prim[i, side, z, q : q + 1, :] for i in (0, 1))
                return fluxes(block, v2, press, lam, 2)

            before = {}

            def emit(i, face):
                before[i] = face
                if i >= 0:
                    rows = pl.ds(8 * (i % 8), 8)
                    acc[z, i // 8, rows, :] += face - before.pop(i - 1)

            stream_faces(load, -1, NY - 1, emit)

            tiles = [
                (halo[stage, 0, z, pl.ds(24, 8), :], halo_prim[0, 0, z]),
                (now[z, 0, pl.ds(64, 8), :], prim[1, 2 * z]),
                (now[z, 1, pl.ds(64, 8), :], prim[1, 2 * z + 1]),
                (halo[stage, 1, z, pl.ds(24, 8), :], halo_prim[0, 1, z]),
            ]
            for index, (block, v2) in enumerate(tiles):
                plus, minus = ninth_fluxes(block, v2, lam)
                for h in range(2):
                    if 0 <= index - h < 3:
                        start = pl.multiple_of(24 * z + 96 * h + 8 * (index - h), 8)
                        ninth_p[pl.ds(start, 8), :] = plus
                        ninth_m[pl.ds(start, 8), :] = minus
            return 0

        lax.fori_loop(0, NZ, transverse, 0)

        before = {}

        def emit_ninth(i, face):
            before[i] = face
            if i >= 0:
                ninth_d[pl.ds(i, 8, stride=8), :] = face - before.pop(i - 1)

        def load_ninth(j):
            rows = pl.ds(8 + j, 8, stride=24)
            return ninth_p[rows, :], ninth_m[rows, :]

        stream_faces(load_ninth, -1, 7, emit_ninth)
        for h in range(2):
            for z in range(NZ):
                acc[z, h, pl.ds(64, 8), :] += ninth_d[pl.ds(8 * (4 * h + z), 8), :]

        keep, blend = STAGES[stage]

        def update(q, _):
            rows = pl.ds(pl.multiple_of(8 * q, 8), 8)
            scale = consts[1] * (blend / 12.0)
            h_low, h_edge = edges[1, rows, :], edges[2, rows, :]
            packed = jnp.zeros((8, LANES), jnp.float32)
            for g in range(GROUPS):
                z, t = g // 2, g % 2
                face = faces[z, t, rows, :]
                face = jnp.where((lane < 2) | (lane > 124), roll(h_edge, -16 * g - 3), face)
                below = jnp.where(lane == 0, roll(h_low, -16 * g - 2), roll(face, 1))
                total = acc[z, t, rows, :] + (face - below)
                value = now[z, t, rows, :]
                if stage > 0:
                    value = keep * fields[0, z, t, rows, :] + blend * value
                value = value - scale * total
                fields[stage + 1, z, t, rows, :] = value
                if stage < 2:
                    here = (lane >> 4) == g
                    ends = jnp.where(place < 8, roll(value, 16 * g + 3), roll(value, 16 * g + 13))
                    packed = jnp.where(here, ends, packed)
            if stage < 2:
                pack[stage + 1, rows, :] = packed
            return 0

        lax.fori_loop(0, BLOCKS, update, 0)

        if stage < 2:
            for copy in y_copies(stage + 1):
                copy.start()
            left, right = x_copies(stage + 1)

            @pl.when(jnp.logical_not(is_last))
            def _():
                left.start()

            @pl.when(me_x > 0)
            def _():
                right.start()

    third = fields.at[3]

    def react(g, _):
        z, t = g // 2, g % 2
        rows = [third[z, t, pl.ds(c, 8, stride=8), :] for c in range(8)]
        rho, m1, m2, m3, energy, reactant, product, other = rows
        inverse = reciprocal(rho)
        rest = energy - 0.5 * (m1 * m1 + m2 * m2 + m3 * m3) * inverse
        small = consts[1] * (PREFACTOR / SUBSTEPS)
        for _ in range(SUBSTEPS):
            press = 0.4 * (rest - reactant)
            burned = small * reactant * jnp.exp(-ACTIVATION * (rho * reciprocal(press)))
            reactant, product = reactant - burned, product + burned
        rows = [rho, m1, m2, m3, energy, reactant, product, other, third[z, t, pl.ds(64, 8), :]]
        for c, value in enumerate(rows):
            result[pl.ds(pl.multiple_of(64 * c + 8 * g, 8), 8), :] = value
        return 0

    lax.fori_loop(0, GROUPS, react, 0)
    deliver = pltpu.make_async_copy(result, out, local_sem.at[0])
    deliver.start()

    for copy in sent_x + sent_y + y_copies(0) + y_copies(1) + y_copies(2):
        copy.wait_send()
    for stage in (1, 2):
        left, right = x_copies(stage)

        @pl.when(jnp.logical_not(is_last))
        def _():
            left.wait_send()

        @pl.when(me_x > 0)
        def _():
            right.wait_send()

    @pl.when(me_x > 0)
    def _():
        shift_copy.wait_send()

    deliver.wait()


def on_device(nx, ny, state, inflow):
    rows = COMPS * NZ * NY
    f32 = jnp.float32

    def vmem(*shape):
        return pltpu.VMEM(shape, f32)

    result = pl.pallas_call(
        functools.partial(kernel, nx, ny),
        out_shape=jax.ShapeDtypeStruct((rows, LANES), f32),
        in_specs=[pl.BlockSpec(memory_space=pl.ANY)] * 2,
        out_specs=pl.BlockSpec(memory_space=pl.ANY),
        scratch_shapes=[
            vmem(rows, LANES),
            vmem(rows, inflow.shape[-1]),
            vmem(rows, LANES),
            vmem(4, NZ, 2, 72, LANES),
            vmem(8, LANES),
            vmem(4, GROUPS, 8, LANES),
            vmem(2, 2, NZ, 8, LANES),
            vmem(NZ, 2, 72, LANES),
            vmem(NZ, 2, 72, LANES),
            vmem(NZ, 2, 72, LANES),
            vmem(NZ, 2, 72, LANES),
            vmem(72, LANES),
            vmem(3, 72, LANES),
            vmem(192, LANES),
            vmem(192, LANES),
            vmem(64, LANES),
            vmem(3, 72, LANES),
            vmem(3, 72, LANES),
            vmem(3, 72, LANES),
            vmem(3, 2, NZ, 32, LANES),
            vmem(8 * 16, LANES),
            vmem(8 * 16, LANES),
            vmem(2, 8, LANES),
            pltpu.SemaphoreType.DMA((2,)),
            pltpu.SemaphoreType.DMA((46,)),
            pltpu.SemaphoreType.DMA((46,)),
        ],
        compiler_params=pltpu.CompilerParams(
            collective_id=0, has_side_effects=True, vmem_limit_bytes=32 * 1024 * 1024
        ),
        cost_estimate=pl.CostEstimate(
            flops=60_000_000, bytes_accessed=1_200_000, transcendentals=5_000_000
        ),
    )(state.reshape(rows, LANES), inflow.reshape(rows, inflow.shape[-1]))
    return result.reshape(state.shape)


def solution(mesh):
    return jax.shard_map(
        functools.partial(on_device, mesh.shape["gx"], mesh.shape["gy"]),
        mesh=mesh,
        in_specs=(P(None, None, "gy", "gx"), P(None, None, "gy", None)),
        out_specs=P(None, None, "gy", "gx"),
        check_vma=False,
    )
```

time: 177 us -> 46 us (0.26)
  the two profiles are of different devices: /device:TPU:24 before, /device:TPU:1 now
where the time goes in v1:
time: 46 us; the launch traced here: 45.9 us
  Pallas kernels  44 us (96%)
  local copies, waits for them, and re-layouts  1.81 us (4%)
    pallas_call x1, Pallas kernels, on_device(): pl.pallas_call(functools.partial(kernel, nx, ny), out_shape=jax.ShapeDtyp...  44 us
    unnamed x4, local copies, waits for them, and re-layouts  1.81 us

profile of v1, /device:TPU:1, one launch (start us, length us, event | category | flops | bytes accessed | tf_op | source)
XLA Modules:
  0.0 45.9 jit_solution(10203139220743850062)
XLA Ops:
  0.0 0.0 copy-start
  0.0 1.1 %copy.3 = f32[9,4,16,8]{3,2,1,0:T(8,128)S(1)} copy(f32[9,4,16,8]{2,3,1,0:T(8,128)} %param.3) | data formatting | bytes 36864 | tf_op args[1]
  1.1 0.0 copy-done
  1.1 44.0 %shard_map.28 = f32[576,128]{1,0:T(8,128)S(1)} custom-call(f32[576,128]{1,0:T(8,128)S(1)} %bitcast.5, f32[576,8]{1,0:T(8,128)S(1)} %bitcast.4), custom_call_target="tpu_custom_call" | custom-call | flops 60000000 | bytes 1200000 | tf_op jit(solution)/shard_map/pallas_call | solution.py:549
  45.2 0.7 %copy.5 = f32[9,4,16,128]{3,2,1,0:T(8,128)} copy(f32[9,4,16,128]{3,2,1,0:T(8,128)S(1)} %bitcast.3) | data formatting | bytes 589824
Async XLA Ops:
  0.0 1.1 %copy-start = (f32[9,4,16,128]{3,2,1,0:T(8,128)S(1)}, f32[9,4,16,128]{3,2,1,0:T(8,128)}, u32[]{:S(2)}) copy-start(f32[9,4,16,128]{3,2,1,0:T(8,128)} %param.2) | copy-start | bytes 884740

commit v2 on v1

--- a/solution.py
+++ b/solution.py
@@ -18,7 +18,7 @@
 PREFACTOR = 300.0
 ACTIVATION = 4.0
 COURANT = 0.15
-EPS = 3e-6
+EPS = 2e-6
 STAGES = ((0.0, 1.0), (0.75, 0.25), (1.0 / 3.0, 2.0 / 3.0))
 
 
@@ -33,12 +33,12 @@
 
 def cell_terms(d_low, d_high, q_low, q_high):
     second = d_high - d_low
-    cross = d_high * d_low
-    squares = (q_low + q_high) + EPS
-    base = squares - 2.75 * cross
-    r_low = reciprocal(base + 1.5 * q_high)
-    r_mid = reciprocal(squares - 1.25 * cross)
-    r_high = reciprocal(base + 1.5 * q_low)
+    half = d_low * (0.5 * d_high)
+    level = (2.0 / 3.0) * (second * second) + EPS
+    base = level - half
+    r_low = reciprocal(base + q_high)
+    r_mid = reciprocal(level + half)
+    r_high = reciprocal(base + q_low)
     return second, r_low * r_low, 6.0 * (r_mid * r_mid), r_high * r_high
 
 
@@ -47,18 +47,15 @@
     return (w_far * t_far + near * (0.5 * t_near)) * reciprocal((w_far + w_mid) + near)
 
 
-def plus_face(g, d_low, d_high, fix):
-    return 6.0 * g + d_low + 2.0 * (d_high - fix)
-
-
-def minus_face(g, d_low, d_high, fix):
-    return 6.0 * g - d_high - 2.0 * (d_low - fix)
+def face_value(gp, gm, dp_low, dp_high, dm_low, dm_high, fix_p, fix_m):
+    inner = (dp_high - dm_low) - (fix_p - fix_m)
+    return 6.0 * (gp + gm) + (dp_low - dm_high) + 2.0 * inner
 
 
 def stream_faces(load, first, last, emit):
     gp, gm, dp, dm, qp, qm = {}, {}, {}, {}, {}, {}
     tp, tm, sp, sm, wp, wm = {}, {}, {}, {}, {}, {}
-    plus = {}
+    fix = {}
     for j in range(first - 2, last + 4):
         gp[j], gm[j] = load(j)
         k = j - 1
@@ -75,12 +72,11 @@
                 tm[k - 1] = sm[k] - sm[k - 1]
             i = k - 1
             if first <= i <= last:
-                fix = correction(wp[i - 1][0], wp[i][1], wp[i + 1][2], tp[i - 1], tp[i])
-                plus[i] = plus_face(gp[i], dp[i - 1], dp[i], fix)
+                fix[i] = correction(wp[i - 1][0], wp[i][1], wp[i + 1][2], tp[i - 1], tp[i])
             i, c = k - 2, k - 1
             if first <= i <= last:
-                fix = correction(wm[c + 1][2], wm[c][1], wm[c - 1][0], tm[c], tm[c - 1])
-                emit(i, plus[i] + minus_face(gm[c], dm[c - 1], dm[c], fix))
+                fix_m = correction(wm[c + 1][2], wm[c][1], wm[c - 1][0], tm[c], tm[c - 1])
+                emit(i, face_value(gp[i], gm[c], dp[i - 1], dp[i], dm[i], dm[c], fix[i], fix_m))
 
 
 def ring_differences(gp, gm):
@@ -100,34 +96,36 @@
         t = [b - a for a, b in zip(s, up(s))]
         return d, t, low, mid, high
 
-    d, t, low, mid, high = parts(gp)
-    fix = [correction(*each) for each in zip(down(low), mid, up(high), down(t), t)]
-    plus = [plus_face(*each) for each in zip(gp, down(d), d, fix)]
-    d, t, low, mid, high = parts(gm)
-    fix = [correction(*each) for each in zip(up(high), mid, down(low), t, down(t))]
-    minus = [minus_face(*each) for each in zip(gm, down(d), d, fix)]
-    faces = [a + b for a, b in zip(plus, up(minus))]
+    dp, t, low, mid, high = parts(gp)
+    fix_p = [correction(*each) for each in zip(down(low), mid, up(high), down(t), t)]
+    dm, t, low, mid, high = parts(gm)
+    fix_m = [correction(*each) for each in zip(up(high), mid, down(low), t, down(t))]
+    faces = [
+        face_value(*each) for each in zip(gp, up(gm), down(dp), dp, dm, up(dm), fix_p, up(fix_m))
+    ]
     return [a - b for a, b in zip(faces, down(faces))]
 
 
-def lane_faces(gp, gm):
-    def up(x):
-        return roll(x, -1)
-
-    def down(x):
-        return roll(x, 1)
-
-    def parts(g):
-        d_high = up(g) - g
-        d_low = down(d_high)
-        second, low, mid, high = cell_terms(d_low, d_high, d_low * d_low, d_high * d_high)
-        return d_low, d_high, up(second) - second, second - down(second), down(low), mid, up(high)
-
-    d_low, d_high, t_up, t_down, low, mid, high = parts(gp)
-    plus = plus_face(gp, d_low, d_high, correction(low, mid, high, t_down, t_up))
-    d_low, d_high, t_up, t_down, low, mid, high = parts(gm)
-    minus = minus_face(gm, d_low, d_high, correction(high, mid, low, t_up, t_down))
-    return plus + up(minus)
+def one_side(far, near, centre, ahead, beyond):
+    d1, d2, d3, d4 = near - far, centre - near, ahead - centre, beyond - ahead
+    q2, q3 = d2 * d2, d3 * d3
+    r_far = reciprocal(d1 * (d1 - 2.75 * d2) + (2.5 * q2 + 1.5 * EPS))
+    r_mid = reciprocal(d2 * (d2 - 1.25 * d3) + (q3 + 1.5 * EPS))
+    r_near = reciprocal(d4 * (d4 - 2.75 * d3) + (2.5 * q3 + 1.5 * EPS))
+    s0, s1, s2 = d2 - d1, d3 - d2, d4 - d3
+    fix = correction(r_far * r_far, 6.0 * (r_mid * r_mid), r_near * r_near, s1 - s0, s2 - s1)
+    return d2, d3, fix
+
+
+def shifted_copies(gp, gm):
+    return [roll(gp, k) for k in (2, 1, 0, -1, -2)] + [roll(gm, k) for k in (-3, -2, -1, 0, 1)]
+
+
+def lane_faces(copies):
+    low, high, fix_p = one_side(*copies[:5])
+    back, front, fix_m = one_side(*copies[5:])
+    inner = (high + front) - (fix_p + fix_m)
+    return 6.0 * (copies[2] + copies[7]) + (low + back) + 2.0 * inner
 
 
 def primitives(rho, m1, m2, m3, energy, reactant):
@@ -146,7 +144,7 @@
 
 def kernel(
     nx, ny, state, inflow, out,
-    raw, infl, result, fields, cells, prim, halo_prim, flux_p, flux_m, acc, faces,
+    raw, infl, turned, fields, prim, halo_prim, lined, acc, faces,
     windows, edges, ninth_p, ninth_m, ninth_d, pack, from_left, from_right, halo, peak_x, peak_y, consts,
     local_sem, send_sem, recv_sem,
 ):
@@ -177,17 +175,34 @@
     fetch_state.wait()
     fetch_inflow.wait()
 
-    def tile_speed(ref, g):
-        rows = [ref[pl.ds(64 * c + 8 * g, 8), :] for c in range(6)]
+    def tile_speed(ref, tile, stride):
+        rows = [ref[pl.ds(stride * c + 8 * tile, 8), :] for c in range(6)]
         return signal_speed(*rows)
 
-    peak = tile_speed(raw, 0)
-    entering = tile_speed(infl, 0)
+    peak = tile_speed(raw, 0, 64)
     for g in range(1, GROUPS):
-        peak = jnp.maximum(peak, tile_speed(raw, g))
-        entering = jnp.maximum(entering, tile_speed(infl, g))
+        peak = jnp.maximum(peak, tile_speed(raw, g, 64))
+    entering = tile_speed(infl, 0, 32)
+    for z in range(1, NZ):
+        entering = jnp.maximum(entering, tile_speed(infl, z, 32))
     peak = jnp.where(is_first & (lane < 8), 0.0, peak)
     peak_x[pl.ds(0, 8), :] = jnp.maximum(peak, jnp.max(entering))
+
+    def opening_block(g, q):
+        if q == 8:
+            return raw[pl.ds(64 * 8 + 8 * g, 8), :]
+        return raw[pl.ds(8 * g + q, 8, stride=64), :]
+
+    for q in range(BLOCKS):
+        head = jnp.zeros((8, LANES), jnp.float32)
+        own = head
+        for g in range(GROUPS):
+            block = opening_block(g, q)
+            here = (lane >> 4) == g
+            head = jnp.where(here, roll(block, 16 * g + 5), head)
+            own = jnp.where(here, roll(block, 16 * g - 5), own)
+        pack[0, pl.ds(8 * q, 8), :] = head
+        windows[pl.ds(8 * q, 8), :] = own
 
     pl.semaphore_wait(barrier, nx + ny - 2)
 
@@ -209,26 +224,6 @@
 
     sent_x = spread(peak_x, nx, 0, lambda k: (k, 0))
 
-    def pack_opening(q, _):
-        head = jnp.zeros((8, LANES), jnp.float32)
-        own = head
-        for g in range(GROUPS):
-            block = opening_block(raw, g, q)
-            here = (lane >> 4) == g
-            head = jnp.where(here, roll(block, 16 * g + 5), head)
-            own = jnp.where(here, roll(block, 16 * g - 5), own)
-        pack[0, pl.ds(pl.multiple_of(8 * q, 8), 8), :] = head
-        windows[pl.ds(pl.multiple_of(8 * q, 8), 8), :] = own
-        return 0
-
-    def opening_block(ref, g, q):
-        if isinstance(q, int) and q == 8:
-            return ref[pl.ds(64 * 8 + 8 * g, 8), :]
-        return ref[pl.ds(8 * g + q, 8, stride=64), :]
-
-    lax.fori_loop(0, 8, pack_opening, 0)
-    pack_opening(8, 0)
-
     shift_copy = remote(pack.at[0], from_right.at[0], 2 * 16, peer(-1, 0))
 
     @pl.when(me_x > 0)
@@ -237,19 +232,18 @@
 
     @pl.when(is_last)
     def _():
-        def pack_inflow(q, _):
+        for c in range(COMPS):
+            turned[pl.ds(16 * c, 16), 0:32] = infl[pl.ds(32 * c, 32), :].T
+        for q in range(BLOCKS):
             head = jnp.zeros((8, LANES), jnp.float32)
             for g in range(GROUPS):
-                block = opening_block(infl, g, q)
-                block = jnp.concatenate([block, jnp.zeros((8, LANES - 8), jnp.float32)], axis=1)
-                head = jnp.where((lane >> 4) == g, roll(block, 16 * g + 5), head)
+                z, t = g // 2, g % 2
+                rows = pl.ds(8 * t + q, 8, stride=16) if q < 8 else pl.ds(128 + 8 * t, 8)
+                block = roll(turned[rows, :], 16 * g + 5 - 8 * z)
+                head = jnp.where((lane >> 4) == g, block, head)
             for k in range(1, 4):
                 head = jnp.where(place == 12 + k, roll(head, k), head)
-            from_right[0, pl.ds(pl.multiple_of(8 * q, 8), 8), :] = head
-            return 0
-
-        lax.fori_loop(0, 8, pack_inflow, 0)
-        pack_inflow(8, 0)
+            from_right[0, pl.ds(8 * q, 8), :] = head
 
     peak_y[pl.ds(0, 8), :] = gather(peak_x, sent_x)
     sent_y = spread(peak_y, ny, 16, lambda k: (0, k))
@@ -258,11 +252,11 @@
     def _():
         shift_copy.wait_recv()
 
-    def assemble(q, _):
-        rows = pl.ds(pl.multiple_of(8 * q, 8), 8)
+    for q in range(BLOCKS):
+        rows = pl.ds(8 * q, 8)
         arrived = from_right[0, rows, :]
         for g in range(GROUPS):
-            block = opening_block(raw, g, q)
+            block = opening_block(g, q)
             block = jnp.where(lane < LANES - 8, roll(block, -8), roll(arrived, 115 - 16 * g))
             fields[0, g // 2, g % 2, rows, :] = block
         own = windows[rows, :]
@@ -271,10 +265,6 @@
             edge = jnp.where(place == 3 - k, roll(own, -k), edge)
         own = jnp.where(is_first, edge, own)
         windows[rows, :] = jnp.where(place < 8, own, arrived)
-        return 0
-
-    lax.fori_loop(0, 8, assemble, 0)
-    assemble(8, 0)
 
     def y_copies(stage):
         now, base = fields.at[stage], 33 + 3 * stage
@@ -314,14 +304,10 @@
         now = fields.at[stage]
         lam = consts[0]
 
-        def own_primitives(g, _):
-            z, t = g // 2, g % 2
-            rows = [now[z, t, pl.ds(c, 8, stride=8), :] for c in range(6)]
+        for g in range(GROUPS):
+            rows = [now[g // 2, g % 2, pl.ds(c, 8, stride=8), :] for c in range(6)]
             for index, value in enumerate(primitives(*rows)):
                 prim[index, g] = value
-            return 0
-
-        lax.fori_loop(0, GROUPS, own_primitives, 0)
 
         def spanwise(t, _):
             for q in range(BLOCKS):
@@ -336,7 +322,8 @@
                     else:
                         one = ninth_fluxes(block, prim[0, 2 * z + t], lam)
                         three = ninth_fluxes(block, prim[2, 2 * z + t], lam)
-                    flux_p[z, t, rows, :], flux_m[z, t, rows, :] = one
+                    for k, value in enumerate(shifted_copies(*one)):
+                        lined[k, z, t, rows, :] = value
                     gp.append(three[0])
                     gm.append(three[1])
                 for z, value in enumerate(ring_differences(gp, gm)):
@@ -349,7 +336,7 @@
             z, t = g // 2, g % 2
             for q in range(BLOCKS):
                 rows = pl.ds(8 * q, 8)
-                faces[z, t, rows, :] = lane_faces(flux_p[z, t, rows, :], flux_m[z, t, rows, :])
+                faces[z, t, rows, :] = lane_faces([lined[k, z, t, rows, :] for k in range(10)])
             return 0
 
         lax.fori_loop(0, GROUPS, streamwise, 0)
@@ -387,9 +374,9 @@
                 pair = fluxes(block, edges[0, q : q + 1, :], edges[0, 8 + q : 9 + q, :], lam, 1)
             else:
                 pair = ninth_fluxes(block, v1, lam)
-            h = lane_faces(*pair)
-            edges[1, rows, :] = h
-            edges[2, rows, :] = jnp.where(place < 3, roll(h, -10), h)
+            face = lane_faces(shifted_copies(*pair))
+            edges[1, rows, :] = jnp.where(place < 3, roll(face, -9), roll(face, 1))
+            edges[2, rows, :] = jnp.where(place < 3, roll(face, -10), face)
 
         for copy in y_copies(stage):
             copy.wait_recv()
@@ -400,6 +387,18 @@
                 start = 5 if side == 0 else 0
                 halo_prim[0, side, z, start : start + 3, :] = v2
                 halo_prim[1, side, z, start : start + 3, :] = press
+
+        def streamwise_difference(z, t, q):
+            rows = pl.ds(8 * q, 8)
+            back = 125 - 32 * z - 16 * t
+            face = faces[z, t, rows, :]
+            under = jnp.where(
+                (lane < 3) | (lane > 125), pltpu.roll(edges[1, rows, :], back, axis=1), roll(face, 1)
+            )
+            face = jnp.where(
+                (lane < 2) | (lane > 124), pltpu.roll(edges[2, rows, :], back, axis=1), face
+            )
+            return face - under
 
         def transverse(z, _):
             def load(j):
@@ -418,10 +417,13 @@
             def emit(i, face):
                 before[i] = face
                 if i >= 0:
-                    rows = pl.ds(8 * (i % 8), 8)
-                    acc[z, i // 8, rows, :] += face - before.pop(i - 1)
+                    t, q = i // 8, i % 8
+                    total = (face - before.pop(i - 1)) + streamwise_difference(z, t, q)
+                    acc[z, t, pl.ds(8 * q, 8), :] += total
 
             stream_faces(load, -1, NY - 1, emit)
+            for t in range(2):
+                acc[z, t, pl.ds(64, 8), :] += streamwise_difference(z, t, 8)
 
             tiles = [
                 (halo[stage, 0, z, pl.ds(24, 8), :], halo_prim[0, 0, z]),
@@ -458,21 +460,16 @@
 
         keep, blend = STAGES[stage]
 
-        def update(q, _):
-            rows = pl.ds(pl.multiple_of(8 * q, 8), 8)
-            scale = consts[1] * (blend / 12.0)
-            h_low, h_edge = edges[1, rows, :], edges[2, rows, :]
+        scale = consts[1] * (blend / 12.0)
+        for q in range(BLOCKS):
+            rows = pl.ds(8 * q, 8)
             packed = jnp.zeros((8, LANES), jnp.float32)
             for g in range(GROUPS):
                 z, t = g // 2, g % 2
-                face = faces[z, t, rows, :]
-                face = jnp.where((lane < 2) | (lane > 124), roll(h_edge, -16 * g - 3), face)
-                below = jnp.where(lane == 0, roll(h_low, -16 * g - 2), roll(face, 1))
-                total = acc[z, t, rows, :] + (face - below)
                 value = now[z, t, rows, :]
                 if stage > 0:
                     value = keep * fields[0, z, t, rows, :] + blend * value
-                value = value - scale * total
+                value = value - scale * acc[z, t, rows, :]
                 fields[stage + 1, z, t, rows, :] = value
                 if stage < 2:
                     here = (lane >> 4) == g
@@ -480,9 +477,6 @@
                     packed = jnp.where(here, ends, packed)
             if stage < 2:
                 pack[stage + 1, rows, :] = packed
-            return 0
-
-        lax.fori_loop(0, BLOCKS, update, 0)
 
         if stage < 2:
             for copy in y_copies(stage + 1):
@@ -499,7 +493,7 @@
 
     third = fields.at[3]
 
-    def react(g, _):
+    for g in range(GROUPS):
         z, t = g // 2, g % 2
         rows = [third[z, t, pl.ds(c, 8, stride=8), :] for c in range(8)]
         rho, m1, m2, m3, energy, reactant, product, other = rows
@@ -512,12 +506,7 @@
             reactant, product = reactant - burned, product + burned
         rows = [rho, m1, m2, m3, energy, reactant, product, other, third[z, t, pl.ds(64, 8), :]]
         for c, value in enumerate(rows):
-            result[pl.ds(pl.multiple_of(64 * c + 8 * g, 8), 8), :] = value
-        return 0
-
-    lax.fori_loop(0, GROUPS, react, 0)
-    deliver = pltpu.make_async_copy(result, out, local_sem.at[0])
-    deliver.start()
+            out[pl.ds(64 * c + 8 * g, 8), :] = value
 
     for copy in sent_x + sent_y + y_copies(0) + y_copies(1) + y_copies(2):
         copy.wait_send()
@@ -536,31 +525,29 @@
     def _():
         shift_copy.wait_send()
 
-    deliver.wait()
-
 
 def on_device(nx, ny, state, inflow):
     rows = COMPS * NZ * NY
     f32 = jnp.float32
 
+    inflow = jnp.swapaxes(inflow, 2, 3).reshape(COMPS * NZ * inflow.shape[3], NY)
+
     def vmem(*shape):
         return pltpu.VMEM(shape, f32)
 
     result = pl.pallas_call(
         functools.partial(kernel, nx, ny),
         out_shape=jax.ShapeDtypeStruct((rows, LANES), f32),
-        in_specs=[pl.BlockSpec(memory_space=pl.ANY)] * 2,
-        out_specs=pl.BlockSpec(memory_space=pl.ANY),
+        in_specs=[pl.BlockSpec(memory_space=pltpu.HBM)] * 2,
+        out_specs=pl.BlockSpec(memory_space=pltpu.VMEM),
         scratch_shapes=[
             vmem(rows, LANES),
-            vmem(rows, inflow.shape[-1]),
-            vmem(rows, LANES),
+            vmem(*inflow.shape),
+            vmem(COMPS * NY, LANES),
             vmem(4, NZ, 2, 72, LANES),
-            vmem(8, LANES),
             vmem(4, GROUPS, 8, LANES),
             vmem(2, 2, NZ, 8, LANES),
-            vmem(NZ, 2, 72, LANES),
-            vmem(NZ, 2, 72, LANES),
+            vmem(10, NZ, 2, 72, LANES),
             vmem(NZ, 2, 72, LANES),
             vmem(NZ, 2, 72, LANES),
             vmem(72, LANES),
@@ -580,12 +567,12 @@
             pltpu.SemaphoreType.DMA((46,)),
         ],
         compiler_params=pltpu.CompilerParams(
-            collective_id=0, has_side_effects=True, vmem_limit_bytes=32 * 1024 * 1024
+            collective_id=0, has_side_effects=True, vmem_limit_bytes=60 * 1024 * 1024
         ),
         cost_estimate=pl.CostEstimate(
             flops=60_000_000, bytes_accessed=1_200_000, transcendentals=5_000_000
         ),
-    )(state.reshape(rows, LANES), inflow.reshape(rows, inflow.shape[-1]))
+    )(state.reshape(rows, LANES), inflow)
     return result.reshape(state.shape)
 
 

time: 46 us -> 38.5 us (0.84)
  Pallas kernels: 44 us -> 36.7 us
    pallas_call x1, Pallas kernels: 44 us -> 36.7 us  [on_device(): pl.pallas_call(functools.partial(kernel, nx, ny), out_shape=jax.ShapeDtyp...]
    unnamed x4 -> x1, local copies, waits for them, and re-layouts: 1.81 us -> 1.69 us
where the time goes in v2:
time: 38.5 us; the launch traced here: 38.4 us
  Pallas kernels  36.7 us (95%)
  local copies, waits for them, and re-layouts  1.69 us (4%)
    pallas_call x1, Pallas kernels, on_device(): pl.pallas_call(functools.partial(kernel, nx, ny), out_shape=jax.ShapeDtyp...  36.7 us
    unnamed x1, local copies, waits for them, and re-layouts  1.69 us

profile of v2, /device:TPU:1, one launch (start us, length us, event | category | flops | bytes accessed | tf_op | source)
XLA Modules:
  0.0 38.4 jit_solution(17572447139064079515)
XLA Ops:
  0.0 36.7 %shard_map.28 = f32[576,128]{1,0:T(8,128)} custom-call(f32[576,128]{1,0:T(8,128)} %bitcast.6, f32[288,16]{1,0:T(8,128)} %bitcast.7), custom_call_target="tpu_custom_call" | custom-call | flops 60000000 | bytes 1200000 | tf_op jit(solution)/shard_map/pallas_call | solution.py:538
  36.7 1.7 %copy.4 = f32[9,4,16,128]{3,2,1,0:T(8,128)} copy(f32[9,4,16,128]{3,2,1,0:T(8,128)} %bitcast.5) | data formatting | bytes 589824

commit v3 on v2

--- a/solution.py
+++ b/solution.py
@@ -128,6 +128,28 @@
     return 6.0 * (copies[2] + copies[7]) + (low + back) + 2.0 * inner
 
 
+def exchange_groups(nx, ny):
+    cores = 2 - nx % 2
+    width = min(4, nx // cores)
+    depth = nx // (cores * width)
+    low = 2 - ny % 2
+    length = ny // low
+    plane, column = [], []
+    for a in range(depth):
+        for b in range(width):
+            for c in range(low):
+                far = min(b, width - b) + (2 if a else c)
+                plane.append((far, (a, b, 0, 0, c)))
+    for d in range(length):
+        for e in range(cores):
+            column.append((min(d, length - d) + 0.2 * e, (0, 0, e, d, 0)))
+    sizes = (depth, width, cores, length, low)
+    plane, column = (
+        [x for x in sorted(group, key=lambda x: -x[0]) if any(x[1])] for group in (plane, column)
+    )
+    return sizes, plane, column
+
+
 def primitives(rho, m1, m2, m3, energy, reactant):
     inverse = reciprocal(rho)
     v1, v2, v3 = m1 * inverse, m2 * inverse, m3 * inverse
@@ -145,7 +167,8 @@
 def kernel(
     nx, ny, state, inflow, out,
     raw, infl, turned, fields, prim, halo_prim, lined, acc, faces,
-    windows, edges, ninth_p, ninth_m, ninth_d, pack, from_left, from_right, halo, peak_x, peak_y, consts,
+    windows, edges, ninth_p, ninth_m, ninth_d, ninth_out, ninth_in, ninth_halo, pack, opening,
+    ends_out, ends_in, halo, peaks, consts,
     local_sem, send_sem, recv_sem,
 ):
     me_x, me_y = lax.axis_index("gx"), lax.axis_index("gy")
@@ -154,8 +177,20 @@
     sub = lax.broadcasted_iota(jnp.int32, (8, LANES), 0)
     place = lane & 15
 
+    sizes, plane, column = exchange_groups(nx, ny)
+    _, n_x, n_core, _, n_low = sizes
+    digits = (
+        me_x // (n_x * n_core), (me_x // n_core) % n_x, me_x % n_core, me_y // n_low, me_y % n_low
+    )
+
     def peer(dx, dy):
         return (lax.rem(me_x + (dx + nx), nx), lax.rem(me_y + (dy + ny), ny))
+
+    def partner(offset):
+        a, b, c, d, e = (
+            x if o == 0 else lax.rem(x + o, n) for x, o, n in zip(digits, offset, sizes)
+        )
+        return ((a * n_x + b) * n_core + c, d * n_low + e)
 
     def remote(src, dst, slot, target):
         return pltpu.make_async_remote_copy(
@@ -168,10 +203,10 @@
     fetch_state.start()
     fetch_inflow.start()
     barrier = pltpu.get_barrier_semaphore()
-    for k in range(1, nx):
-        pl.semaphore_signal(barrier, inc=1, device_id=peer(k, 0), device_id_type=MESH)
-    for k in range(1, ny):
-        pl.semaphore_signal(barrier, inc=1, device_id=peer(0, k), device_id_type=MESH)
+    greeted = [partner(offset) for _, offset in sorted(plane + column, key=lambda x: -x[0])]
+    greeted += [peer(1, 0), peer(-1, 0), peer(0, 1), peer(0, -1)]
+    for device in greeted:
+        pl.semaphore_signal(barrier, inc=1, device_id=device, device_id_type=MESH)
     fetch_state.wait()
     fetch_inflow.wait()
 
@@ -186,7 +221,27 @@
     for z in range(1, NZ):
         entering = jnp.maximum(entering, tile_speed(infl, z, 32))
     peak = jnp.where(is_first & (lane < 8), 0.0, peak)
-    peak_x[pl.ds(0, 8), :] = jnp.maximum(peak, jnp.max(entering))
+    top = jnp.maximum(jnp.max(peak), jnp.max(entering))
+    peaks[0, 0:1, :] = jnp.full((1, LANES), top, jnp.float32)
+
+    pl.semaphore_wait(barrier, len(greeted))
+
+    def phase_copy(phase, rows, device):
+        return remote(
+            peaks.at[phase, pl.ds(0, rows)], peaks.at[phase, pl.ds(1, rows)], phase, device
+        )
+
+    def send_peak(phase, group):
+        for k, (_, offset) in enumerate(group):
+            remote(
+                peaks.at[phase, pl.ds(0, 1)], peaks.at[phase, pl.ds(k + 1, 1)], phase, partner(offset)
+            ).start()
+
+    def largest(phase, group):
+        phase_copy(phase, len(group), partner(group[0][1])).wait_recv()
+        return jnp.max(peaks[phase, pl.ds(0, len(group) + 1), :], axis=0, keepdims=True)
+
+    send_peak(0, plane)
 
     def opening_block(g, q):
         if q == 8:
@@ -204,27 +259,7 @@
         pack[0, pl.ds(8 * q, 8), :] = head
         windows[pl.ds(8 * q, 8), :] = own
 
-    pl.semaphore_wait(barrier, nx + ny - 2)
-
-    def spread(buffer, count, base, step):
-        copies = []
-        for k in range(1, count):
-            copies.append(
-                remote(buffer.at[pl.ds(0, 8)], buffer.at[pl.ds(8 * k, 8)], base + k, peer(*step(k)))
-            )
-            copies[-1].start()
-        return copies
-
-    def gather(buffer, copies):
-        total = buffer[pl.ds(0, 8), :]
-        for k, copy in enumerate(copies):
-            copy.wait_recv()
-            total = jnp.maximum(total, buffer[pl.ds(8 * (k + 1), 8), :])
-        return total
-
-    sent_x = spread(peak_x, nx, 0, lambda k: (k, 0))
-
-    shift_copy = remote(pack.at[0], from_right.at[0], 2 * 16, peer(-1, 0))
+    shift_copy = remote(pack.at[0, pl.ds(0, 72)], opening, 2, peer(-1, 0))
 
     @pl.when(me_x > 0)
     def _():
@@ -243,10 +278,10 @@
                 head = jnp.where((lane >> 4) == g, block, head)
             for k in range(1, 4):
                 head = jnp.where(place == 12 + k, roll(head, k), head)
-            from_right[0, pl.ds(8 * q, 8), :] = head
-
-    peak_y[pl.ds(0, 8), :] = gather(peak_x, sent_x)
-    sent_y = spread(peak_y, ny, 16, lambda k: (0, k))
+            opening[pl.ds(8 * q, 8), :] = head
+
+    peaks[1, 0:1, :] = largest(0, plane)
+    send_peak(1, column)
 
     @pl.when(jnp.logical_not(is_last))
     def _():
@@ -254,7 +289,7 @@
 
     for q in range(BLOCKS):
         rows = pl.ds(8 * q, 8)
-        arrived = from_right[0, rows, :]
+        arrived = opening[rows, :]
         for g in range(GROUPS):
             block = opening_block(g, q)
             block = jnp.where(lane < LANES - 8, roll(block, -8), roll(arrived, 115 - 16 * g))
@@ -266,29 +301,31 @@
         own = jnp.where(is_first, edge, own)
         windows[rows, :] = jnp.where(place < 8, own, arrived)
 
+    def pack_ninth(stage):
+        for z in range(NZ):
+            ninth_out[stage, 0, 4 * z : 4 * z + 3, :] = fields[stage, z, 1, 69:72, :]
+            ninth_out[stage, 1, 4 * z : 4 * z + 3, :] = fields[stage, z, 0, 64:67, :]
+
     def y_copies(stage):
-        now, base = fields.at[stage], 33 + 3 * stage
-        low, high = halo.at[stage, 0], halo.at[stage, 1]
+        now, base = fields.at[stage], 3 + 4 * stage
+        up, down = peer(0, 1), peer(0, -1)
         return [
-            remote(now.at[:, 1, 40:72, :], low, base, peer(0, 1)),
-            remote(now.at[:, 0, 0:24, :], high.at[:, 0:24, :], base + 1, peer(0, -1)),
-            remote(now.at[:, 0, 64:72, :], high.at[:, 24:32, :], base + 2, peer(0, -1)),
+            remote(now.at[:, 1, 40:64, :], halo.at[stage, 0], base, up),
+            remote(now.at[:, 0, 0:24, :], halo.at[stage, 1], base + 1, down),
+            remote(ninth_out.at[stage, 0], ninth_in.at[stage, 0], base + 2, up),
+            remote(ninth_out.at[stage, 1], ninth_in.at[stage, 1], base + 3, down),
         ]
 
     def x_copies(stage):
-        base = 42 + 2 * (stage - 1)
+        base = 15 + 2 * (stage - 1)
         return [
-            remote(pack.at[stage], from_left.at[stage], base, peer(1, 0)),
-            remote(pack.at[stage], from_right.at[stage], base + 1, peer(-1, 0)),
+            remote(ends_out.at[stage - 1, 0], ends_in.at[stage - 1, 0], base, peer(1, 0)),
+            remote(ends_out.at[stage - 1, 1], ends_in.at[stage - 1, 1], base + 1, peer(-1, 0)),
         ]
 
+    pack_ninth(0)
     for copy in y_copies(0):
         copy.start()
-
-    top = jnp.max(gather(peak_y, sent_y))
-    speed = jnp.full((8, LANES), top, jnp.float32)
-    consts[0] = speed
-    consts[1] = COURANT / speed
 
     def fluxes(block, velocity, press, lam, component):
         flow = velocity * (block + jnp.where(sub == 4, press, 0.0))
@@ -302,12 +339,16 @@
 
     for stage in range(3):
         now = fields.at[stage]
-        lam = consts[0]
-
         for g in range(GROUPS):
             rows = [now[g // 2, g % 2, pl.ds(c, 8, stride=8), :] for c in range(6)]
             for index, value in enumerate(primitives(*rows)):
                 prim[index, g] = value
+
+        if stage == 0:
+            speed = jnp.broadcast_to(largest(1, column), (8, LANES))
+            consts[0] = speed
+            consts[1] = COURANT / speed
+        lam = consts[0]
 
         def spanwise(t, _):
             for q in range(BLOCKS):
@@ -359,8 +400,9 @@
                 for k in range(1, 4):
                     low = jnp.where(place == 3 - k, roll(own, -k), low)
                     high = jnp.where(place == 12 + k, roll(own, k), high)
-                low = jnp.where(is_first, low, from_left[stage, rows, :])
-                high = jnp.where(is_last, high, from_right[stage, rows, :])
+                tile, at = pl.ds(8 * (q // 5), 8), 3 * (q % 5)
+                low = jnp.where(is_first, low, roll(ends_in[stage - 1, 0, tile, :], -at))
+                high = jnp.where(is_last, high, roll(ends_in[stage - 1, 1, tile, :], 13 - at))
                 windows[rows, :] = jnp.where(place < 3, low, jnp.where(place > 12, high, own))
 
         rows6 = [windows[pl.ds(c, 8, stride=8), :] for c in range(6)]
@@ -387,6 +429,7 @@
                 start = 5 if side == 0 else 0
                 halo_prim[0, side, z, start : start + 3, :] = v2
                 halo_prim[1, side, z, start : start + 3, :] = press
+                ninth_halo[side, z, start : start + 3, :] = ninth_in[stage, side, 4 * z : 4 * z + 3, :]
 
         def streamwise_difference(z, t, q):
             rows = pl.ds(8 * q, 8)
@@ -426,10 +469,10 @@
                 acc[z, t, pl.ds(64, 8), :] += streamwise_difference(z, t, 8)
 
             tiles = [
-                (halo[stage, 0, z, pl.ds(24, 8), :], halo_prim[0, 0, z]),
+                (ninth_halo[0, z], halo_prim[0, 0, z]),
                 (now[z, 0, pl.ds(64, 8), :], prim[1, 2 * z]),
                 (now[z, 1, pl.ds(64, 8), :], prim[1, 2 * z + 1]),
-                (halo[stage, 1, z, pl.ds(24, 8), :], halo_prim[0, 1, z]),
+                (ninth_halo[1, z], halo_prim[0, 1, z]),
             ]
             for index, (block, v2) in enumerate(tiles):
                 plus, minus = ninth_fluxes(block, v2, lam)
@@ -461,16 +504,31 @@
         keep, blend = STAGES[stage]
 
         scale = consts[1] * (blend / 12.0)
+
+        def update(q, z, t):
+            rows = pl.ds(8 * q, 8)
+            value = now[z, t, rows, :]
+            if stage > 0:
+                value = keep * fields[0, z, t, rows, :] + blend * value
+            value = value - scale * acc[z, t, rows, :]
+            fields[stage + 1, z, t, rows, :] = value
+            return value
+
+        outer = [(0, 0), (1, 0), (2, 0), (8, 0), (5, 1), (6, 1), (7, 1), (8, 1)]
+        for q, t in outer:
+            for z in range(NZ):
+                update(q, z, t)
+        if stage < 2:
+            pack_ninth(stage + 1)
+            for copy in y_copies(stage + 1):
+                copy.start()
+
         for q in range(BLOCKS):
             rows = pl.ds(8 * q, 8)
             packed = jnp.zeros((8, LANES), jnp.float32)
             for g in range(GROUPS):
                 z, t = g // 2, g % 2
-                value = now[z, t, rows, :]
-                if stage > 0:
-                    value = keep * fields[0, z, t, rows, :] + blend * value
-                value = value - scale * acc[z, t, rows, :]
-                fields[stage + 1, z, t, rows, :] = value
+                value = fields[stage + 1, z, t, rows, :] if (q, t) in outer else update(q, z, t)
                 if stage < 2:
                     here = (lane >> 4) == g
                     ends = jnp.where(place < 8, roll(value, 16 * g + 3), roll(value, 16 * g + 13))
@@ -478,9 +536,18 @@
             if stage < 2:
                 pack[stage + 1, rows, :] = packed
 
+        def pack_ends(tile, _):
+            for side in range(2):
+                joined = jnp.zeros((8, LANES), jnp.float32)
+                for k in range(5):
+                    window = pack[stage + 1, pl.ds(pl.multiple_of(40 * tile + 8 * k, 8), 8), :]
+                    moved = roll(window, 3 * k - 13 * side)
+                    joined = jnp.where((place >= 3 * k) & (place < 3 * k + 3), moved, joined)
+                ends_out[stage, side, pl.ds(pl.multiple_of(8 * tile, 8), 8), :] = joined
+            return 0
+
         if stage < 2:
-            for copy in y_copies(stage + 1):
-                copy.start()
+            lax.fori_loop(0, 2, pack_ends, 0)
             left, right = x_copies(stage + 1)
 
             @pl.when(jnp.logical_not(is_last))
@@ -508,7 +575,9 @@
         for c, value in enumerate(rows):
             out[pl.ds(64 * c + 8 * g, 8), :] = value
 
-    for copy in sent_x + sent_y + y_copies(0) + y_copies(1) + y_copies(2):
+    for phase, group in enumerate((plane, column)):
+        phase_copy(phase, len(group), partner(group[0][1])).wait_send()
+    for copy in y_copies(0) + y_copies(1) + y_copies(2):
         copy.wait_send()
     for stage in (1, 2):
         left, right = x_copies(stage)
@@ -555,19 +624,22 @@
             vmem(192, LANES),
             vmem(192, LANES),
             vmem(64, LANES),
-            vmem(3, 72, LANES),
-            vmem(3, 72, LANES),
-            vmem(3, 72, LANES),
-            vmem(3, 2, NZ, 32, LANES),
-            vmem(8 * 16, LANES),
-            vmem(8 * 16, LANES),
+            vmem(3, 2, 16, LANES),
+            vmem(3, 2, 16, LANES),
+            vmem(2, NZ, 8, LANES),
+            vmem(3, 80, LANES),
+            vmem(72, LANES),
+            vmem(2, 2, 16, LANES),
+            vmem(2, 2, 16, LANES),
+            vmem(3, 2, NZ, 24, LANES),
+            vmem(2, 32, LANES),
             vmem(2, 8, LANES),
             pltpu.SemaphoreType.DMA((2,)),
-            pltpu.SemaphoreType.DMA((46,)),
-            pltpu.SemaphoreType.DMA((46,)),
+            pltpu.SemaphoreType.DMA((20,)),
+            pltpu.SemaphoreType.DMA((20,)),
         ],
         compiler_params=pltpu.CompilerParams(
-            collective_id=0, has_side_effects=True, vmem_limit_bytes=60 * 1024 * 1024
+            collective_id=0, has_side_effects=True, vmem_limit_bytes=32 * 1024 * 1024
         ),
         cost_estimate=pl.CostEstimate(
             flops=60_000_000, bytes_accessed=1_200_000, transcendentals=5_000_000

time: 38.5 us -> 36.3 us (0.943)
  Pallas kernels: 36.7 us -> 33.6 us
  local copies, waits for them, and re-layouts: 1.69 us -> 2.59 us
    pallas_call x1, Pallas kernels: 36.7 us -> 33.6 us  [on_device(): pl.pallas_call(functools.partial(kernel, nx, ny), out_shape=jax.ShapeDtyp...]
    unnamed x1 -> x5, local copies, waits for them, and re-layouts: 1.69 us -> 2.59 us
where the time goes in v3:
time: 36.3 us; the launch traced here: 36.2 us
  Pallas kernels  33.6 us (93%)
  local copies, waits for them, and re-layouts  2.59 us (7%)
    pallas_call x1, Pallas kernels, on_device(): pl.pallas_call(functools.partial(kernel, nx, ny), out_shape=jax.ShapeDtyp...  33.6 us
    unnamed x5, local copies, waits for them, and re-layouts  2.59 us

profile of v3, /device:TPU:1, one launch (start us, length us, event | category | flops | bytes accessed | tf_op | source)
XLA Modules:
  0.0 36.2 jit_solution(7275865708126885881)
XLA Ops:
  0.0 0.0 copy-start
  0.0 1.0 %copy-done = f32[9,4,16,128]{3,2,1,0:T(8,128)S(1)} copy-done((f32[9,4,16,128]{3,2,1,0:T(8,128)S(1)}, f32[9,4,16,128]{3,2,1,0:T(8,128)}, u32[]{:S(2)}) %copy-start) | copy-done | bytes 294936
  1.0 0.0 copy-start.1
  1.0 0.9 %copy-done.1 = f32[9,4,16,8]{2,3,1,0:T(8,128)S(1)} copy-done((f32[9,4,16,8]{2,3,1,0:T(8,128)S(1)}, f32[9,4,16,8]{2,3,1,0:T(8,128)}, u32[]{:S(2)}) %copy-start.1) | copy-done | bytes 18456
  1.9 33.6 %shard_map.28 = f32[576,128]{1,0:T(8,128)S(1)} custom-call(f32[576,128]{1,0:T(8,128)S(1)} %bitcast.6, f32[288,16]{1,0:T(8,128)S(1)} %bitcast.7), custom_call_target="tpu_custom_call" | custom-call | flops 60000000 | bytes 1200000 | tf_op jit(solution)/shard_map/pallas_call | solution.py:607
  35.5 0.7 %copy.4 = f32[9,4,16,128]{3,2,1,0:T(8,128)} copy(f32[9,4,16,128]{3,2,1,0:T(8,128)S(1)} %bitcast.5) | data formatting | bytes 589824
Async XLA Ops:
  0.0 1.0 %copy-start = (f32[9,4,16,128]{3,2,1,0:T(8,128)S(1)}, f32[9,4,16,128]{3,2,1,0:T(8,128)}, u32[]{:S(2)}) copy-start(f32[9,4,16,128]{3,2,1,0:T(8,128)} %param.2) | copy-start | bytes 884740
  1.0 0.9 %copy-start.1 = (f32[9,4,16,8]{2,3,1,0:T(8,128)S(1)}, f32[9,4,16,8]{2,3,1,0:T(8,128)}, u32[]{:S(2)}) copy-start(f32[9,4,16,8]{2,3,1,0:T(8,128)} %param.3) | copy-start | bytes 55300

commit v4 on v3

--- a/solution.py
+++ b/solution.py
@@ -639,7 +639,7 @@
             pltpu.SemaphoreType.DMA((20,)),
         ],
         compiler_params=pltpu.CompilerParams(
-            collective_id=0, has_side_effects=True, vmem_limit_bytes=32 * 1024 * 1024
+            collective_id=0, has_side_effects=True, vmem_limit_bytes=54720 * 1024
         ),
         cost_estimate=pl.CostEstimate(
             flops=60_000_000, bytes_accessed=1_200_000, transcendentals=5_000_000

time: 36.3 us -> 35.3 us (0.972)
  local copies, waits for them, and re-layouts: 2.59 us -> 1.63 us
    unnamed x5 -> x3, local copies, waits for them, and re-layouts: 2.59 us -> 1.63 us
where the time goes in v4:
time: 35.3 us; the launch traced here: 35.2 us
  Pallas kernels  33.5 us (95%)
  local copies, waits for them, and re-layouts  1.63 us (5%)
    pallas_call x1, Pallas kernels, on_device(): pl.pallas_call(functools.partial(kernel, nx, ny), out_shape=jax.ShapeDtyp...  33.5 us
    unnamed x3, local copies, waits for them, and re-layouts  1.63 us

profile of v4, /device:TPU:1, one launch (start us, length us, event | category | flops | bytes accessed | tf_op | source)
XLA Modules:
  0.0 35.2 jit_solution(10960279902393547073)
XLA Ops:
  0.0 0.0 copy-start
  0.0 0.9 %copy-done = f32[9,4,16,8]{2,3,1,0:T(8,128)S(1)} copy-done((f32[9,4,16,8]{2,3,1,0:T(8,128)S(1)}, f32[9,4,16,8]{2,3,1,0:T(8,128)}, u32[]{:S(2)}) %copy-start) | copy-done | bytes 18456
  0.9 33.5 %shard_map.28 = f32[576,128]{1,0:T(8,128)S(1)} custom-call(f32[576,128]{1,0:T(8,128)} %bitcast.7, f32[288,16]{1,0:T(8,128)S(1)} %bitcast.6), custom_call_target="tpu_custom_call" | custom-call | flops 60000000 | bytes 1200000 | tf_op jit(solution)/shard_map/pallas_call | solution.py:607
  34.5 0.7 %copy.4 = f32[9,4,16,128]{3,2,1,0:T(8,128)} copy(f32[9,4,16,128]{3,2,1,0:T(8,128)S(1)} %bitcast.5) | data formatting | bytes 589824
Async XLA Ops:
  0.0 0.9 %copy-start = (f32[9,4,16,8]{2,3,1,0:T(8,128)S(1)}, f32[9,4,16,8]{2,3,1,0:T(8,128)}, u32[]{:S(2)}) copy-start(f32[9,4,16,8]{2,3,1,0:T(8,128)} %param.3) | copy-start | bytes 55300

commit v5 on v4

--- a/solution.py
+++ b/solution.py
@@ -420,6 +420,26 @@
             edges[1, rows, :] = jnp.where(place < 3, roll(face, -9), roll(face, 1))
             edges[2, rows, :] = jnp.where(place < 3, roll(face, -10), face)
 
+        if stage == 2:
+            for phase, group in enumerate((plane, column)):
+                phase_copy(phase, len(group), partner(group[0][1])).wait_send()
+            for copy in y_copies(0) + y_copies(1) + y_copies(2):
+                copy.wait_send()
+            for later in (1, 2):
+                left, right = x_copies(later)
+
+                @pl.when(jnp.logical_not(is_last))
+                def _():
+                    left.wait_send()
+
+                @pl.when(me_x > 0)
+                def _():
+                    right.wait_send()
+
+            @pl.when(me_x > 0)
+            def _():
+                shift_copy.wait_send()
+
         for copy in y_copies(stage):
             copy.wait_recv()
         for side in range(2):
@@ -574,25 +594,6 @@
         rows = [rho, m1, m2, m3, energy, reactant, product, other, third[z, t, pl.ds(64, 8), :]]
         for c, value in enumerate(rows):
             out[pl.ds(64 * c + 8 * g, 8), :] = value
-
-    for phase, group in enumerate((plane, column)):
-        phase_copy(phase, len(group), partner(group[0][1])).wait_send()
-    for copy in y_copies(0) + y_copies(1) + y_copies(2):
-        copy.wait_send()
-    for stage in (1, 2):
-        left, right = x_copies(stage)
-
-        @pl.when(jnp.logical_not(is_last))
-        def _():
-            left.wait_send()
-
-        @pl.when(me_x > 0)
-        def _():
-            right.wait_send()
-
-    @pl.when(me_x > 0)
-    def _():
-        shift_copy.wait_send()
 
 
 def on_device(nx, ny, state, inflow):

time: 35.3 us -> 35.3 us (level)
  no operation moved by 1% of the time
where the time goes in v5:
time: 35.3 us; the launch traced here: 35.2 us
  Pallas kernels  33.5 us (95%)
  local copies, waits for them, and re-layouts  1.63 us (5%)
    pallas_call x1, Pallas kernels, on_device(): pl.pallas_call(functools.partial(kernel, nx, ny), out_shape=jax.ShapeDtyp...  33.5 us
    unnamed x3, local copies, waits for them, and re-layouts  1.63 us

profile of v5, /device:TPU:1, one launch (start us, length us, event | category | flops | bytes accessed | tf_op | source)
XLA Modules:
  0.0 35.2 jit_solution(2868041067679351265)
XLA Ops:
  0.0 0.0 copy-start
  0.0 0.9 %copy-done = f32[9,4,16,8]{2,3,1,0:T(8,128)S(1)} copy-done((f32[9,4,16,8]{2,3,1,0:T(8,128)S(1)}, f32[9,4,16,8]{2,3,1,0:T(8,128)}, u32[]{:S(2)}) %copy-start) | copy-done | bytes 18456
  0.9 33.5 %shard_map.28 = f32[576,128]{1,0:T(8,128)S(1)} custom-call(f32[576,128]{1,0:T(8,128)} %bitcast.7, f32[288,16]{1,0:T(8,128)S(1)} %bitcast.6), custom_call_target="tpu_custom_call" | custom-call | flops 60000000 | bytes 1200000 | tf_op jit(solution)/shard_map/pallas_call | solution.py:608
  34.4 0.7 %copy.4 = f32[9,4,16,128]{3,2,1,0:T(8,128)} copy(f32[9,4,16,128]{3,2,1,0:T(8,128)S(1)} %bitcast.5) | data formatting | bytes 589824
Async XLA Ops:
  0.0 0.9 %copy-start = (f32[9,4,16,8]{2,3,1,0:T(8,128)S(1)}, f32[9,4,16,8]{2,3,1,0:T(8,128)}, u32[]{:S(2)}) copy-start(f32[9,4,16,8]{2,3,1,0:T(8,128)} %param.3) | copy-start | bytes 55300
